TPU v7x, 256 devices: a whole 4x4x8 slice. The times are simulated.
256 devices in a mesh: tm: 64 (over z, y_hi, x), sta: 4 (over y_lo, core).
Axes of the slice: x: 4, y: 4 (y_hi: 2, y_lo: 2; y = y_hi * 2 + y_lo), z: 8, core: 2. Of those that a mesh axis runs over, the one named last changes fastest.
Arguments:
- data: bfloat16 [288, 131072], P('sta', 'tm'), may hold values from -6 to 6
- bank: bfloat16 [64, 288, 1024], P('tm', 'sta'), may hold values from -6 to 6
- select: int32 [4], replicated, may hold values from 0 to 63
- shifts: int32 [4, 288], P(None, 'sta'), may hold values from 0 to 255
Outputs:
- detection: float32 [4, 131072], P('sta', 'tm')
All inputs are finite; a program needn't handle non-finite values. Where the computation divides by a largest or mean magnitude, that divisor is 1e-20 or more.
Results may differ from a plain program's by a relative error of at most 0.0029.
Values may be sent and summed in bfloat16 or wider, within the bound.
A program may use at most 64 MiB of HBM per device.

v0:
```python
import jax
import jax.numpy as jnp
from jax import lax
from jax.sharding import PartitionSpec as P

TL = 1024
MAXSHIFT = 256


group_width = 4


def passed_along(value, axis, steps):
    count = lax.axis_size(axis)
    initial, last = (max(0, -steps), min(count, count - steps))
    return lax.ppermute(value, axis, [(source, source + steps) for source in range(initial, last)])


def broadcast(block, axis, owner):
    block = jnp.where(lax.axis_index(axis) == owner, block, jnp.zeros_like(block))
    return lax.psum(block, axis)


def window_sums(values, out_length):
    width = 32
    span = TL // width
    nblocks = (out_length + TL) // width
    starts = out_length // width
    lead = values.shape[:-1]
    blocks = values.reshape(lead + (nblocks, width))
    inner_sums = jnp.cumsum(blocks, axis=-1) - blocks
    block_totals = jnp.sum(blocks, axis=-1)
    running = jnp.concatenate(
        [jnp.zeros(lead + (1,), jnp.float32), jnp.cumsum(block_totals, axis=-1)], axis=-1
    )
    whole_span = running[..., span : span + starts] - running[..., :starts]
    result = (
        whole_span[..., None]
        - inner_sums[..., :starts, :]
        + inner_sums[..., span : span + starts, :]
    )
    return result.reshape(lead + (out_length,))


def normalize_templates(rows):
    centred = rows - jnp.mean(rows, axis=-1, keepdims=True)
    factor = lax.rsqrt(jnp.sum(centred * centred, axis=-1, keepdims=True) + 1e-05)
    return (centred * factor).astype(jnp.bfloat16)


def on_device(data, bank, select, shifts):
    channels, samples = data.shape
    templates = select.shape[0]
    reach = TL + MAXSHIFT
    following = passed_along(data[:, :reach], "tm", -1)
    extended = jnp.concatenate([data, following], axis=1)
    fetched = jnp.stack([broadcast(bank[0], "tm", select[k]) for k in range(templates)], axis=0)
    normed = normalize_templates(fetched.astype(jnp.float32))
    out_length = samples + MAXSHIFT
    starts = out_length // 32
    lag_count = TL // 32 + 1
    lag_padded = (lag_count + 3) // 4 * 4
    spread_width = lag_padded * 32
    groups = channels // group_width
    data_groups = extended.reshape(groups, group_width, extended.shape[1])
    tpl_groups = normed.reshape(templates, groups, group_width, TL).transpose(1, 2, 0, 3)
    shift_groups = shifts.reshape(templates, groups, group_width).transpose(1, 0, 2)

    def group_step(carried, pieces):
        data_part, tpl_part, shift_part = pieces
        as_float = data_part.astype(jnp.float32)
        window_sum = window_sums(as_float, out_length)
        window_sq = window_sums(as_float * as_float, out_length)
        scale_rows = lax.rsqrt(jnp.maximum(window_sq - window_sum * window_sum / TL, TL / 8.0))
        padded = jnp.pad(data_part, ((0, 0), (0, (lag_padded - lag_count) * 32)))
        blocked = padded.reshape(group_width, starts + lag_padded - 1, 32)
        windows = jnp.concatenate(
            [blocked[:, q : q + starts, :] for q in range(lag_padded)], axis=2
        )
        tpl_pad = jnp.pad(tpl_part, ((0, 0), (0, 0), (32, spread_width - TL)))
        spread = jnp.stack(
            [tpl_pad[:, :, 32 - r : 32 - r + spread_width] for r in range(32)], axis=2
        )
        spread = spread.reshape(group_width, templates * 32, spread_width)
        correl = jnp.einsum("cam,cnm->can", windows, spread, preferred_element_type=jnp.float32)
        correl = correl.reshape(group_width, starts, templates, 32).transpose(2, 0, 1, 3)
        correl = correl.reshape(templates, group_width, out_length) * scale_rows[None]
        moved = jax.vmap(
            jax.vmap(lambda series, offset: lax.dynamic_slice_in_dim(series, offset, samples))
        )(correl, shift_part)
        return (carried + jnp.sum(moved, axis=1), None)

    initial = jnp.zeros((templates, samples), jnp.float32)
    partial_stack, _ = lax.scan(group_step, initial, (data_groups, tpl_groups, shift_groups))
    summed = lax.psum(partial_stack, "sta")
    peaks = lax.pmax(jnp.max(jnp.abs(summed), axis=1), "tm")
    rows_each = templates // lax.axis_size("sta")
    first_row = lax.axis_index("sta") * rows_each
    mine = lax.dynamic_slice_in_dim(summed, first_row, rows_each, 0)
    peak_mine = lax.dynamic_slice_in_dim(peaks, first_row, rows_each, 0)
    return mine / (peak_mine[:, None] + 1e-06)


def solution(mesh):
    in_specs = (P("sta", "tm"), P("tm", "sta", None), P(), P(None, "sta"))
    out_specs = P("sta", "tm")
    return jax.shard_map(
        on_device, mesh=mesh, in_specs=in_specs, out_specs=out_specs, check_vma=False
    )
```

profile of v0, /device:TPU:1, one launch (start us, length us, event | category | flops | bytes accessed | tf_op | source)
XLA Modules:
  0.0 1870.2 jit_solution(16156026939483056342)
XLA Ops:
  14.9 627.0 %all-reduce.7.cloned.1.call-done = (bf16[72,1024]{1,0:T(8,128)(2,1)}, bf16[72,1024]{1,0:T(8,128)(2,1)}, bf16[72,1024]{1,0:T(8,128)(2,1)}, bf16[72,1024]{1,0:T(8,128)(2,1)}) async-done(((bf16[72,1024]{1,0:T(8,128)(2,1)}, bf16[72,1024]{1,0:T(8,128)(2,1)}, bf16[72,1024]{1,0:T(8,128)(2,1)}, bf16[72,1024]{1,0:T(8,128)(2,1)}), (bf16[72,1024]{1,0:T(8,128)(2,1)}, bf16[72,1024]{1,0:T(8,128)(2,1)}, ...) | async-done | bytes 589840 | tf_op jit(solution)/shard_map/psum | solution.py:21
  647.8 1020.5 %while.17 = (s32[]{:T(128)}, f32[4,2048]{1,0:T(4,128)S(1)}, bf16[18,4,3328]{2,1,0:T(4,128)(2,1)S(1)}, bf16[18,4,4,1024]{3,1,0,2:T(4,128)(2,1)}, s32[18,4,4]{2,0,...) while((s32[]{:T(128)}, f32[4,2048]{1,0:T(4,128)S(1)}, ...), condition=%wide.region_14.15_spmd.clone, body=%wide.region_6.14_spmd.clone.sunk | while | flops 86090320 | bytes 16013346 | solution.py:94
  659.5 44.9 %while.18 = (s32[]{:T(128)}, f32[4,4,2304]{2,1,0:T(4,128)S(1)}, s32[16,3]{0,1:T(4,128)S(1)}, f32[16,2048]{1,0:T(8,128)S(1)}, s32[]{:T(128)}, /*index=5*/s32[]{:T(128)}) while((s32[]{:T(128)}, f32[4,4,2304]{2,1,0:T(4,128)S(1)}, s32[16,3]{0,1:T(4,128)S(1)}, f32[16,2048]{1,0:T(8,128)S(1)}, s32[]{:T(128)}, /*index=5*/s32[]{:T(128)}) %tuple.116), condition=%wide.while_cond, body=%wide.while_body.sunk | while | flops 2 | bytes 32913 | solution.py:89
  693.8 1.9 dynamic-slice_bitcast_fusion.3
  716.2 44.9 %while.18 = (s32[]{:T(128)}, f32[4,4,2304]{2,1,0:T(4,128)S(1)}, s32[16,3]{0,1:T(4,128)S(1)}, f32[16,2048]{1,0:T(8,128)S(1)}, s32[]{:T(128)}, /*index=5*/s32[]{:T(128)}) while((s32[]{:T(128)}, f32[4,4,2304]{2,1,0:T(4,128)S(1)}, s32[16,3]{0,1:T(4,128)S(1)}, f32[16,2048]{1,0:T(8,128)S(1)}, s32[]{:T(128)}, /*index=5*/s32[]{:T(128)}) %tuple.116), condition=%wide.while_cond, body=%wide.while_body.sunk | while | flops 2 | bytes 32913 | solution.py:89
  739.3 1.9 dynamic-slice_bitcast_fusion.3
  772.8 44.9 %while.18 = (s32[]{:T(128)}, f32[4,4,2304]{2,1,0:T(4,128)S(1)}, s32[16,3]{0,1:T(4,128)S(1)}, f32[16,2048]{1,0:T(8,128)S(1)}, s32[]{:T(128)}, /*index=5*/s32[]{:T(128)}) while((s32[]{:T(128)}, f32[4,4,2304]{2,1,0:T(4,128)S(1)}, s32[16,3]{0,1:T(4,128)S(1)}, f32[16,2048]{1,0:T(8,128)S(1)}, s32[]{:T(128)}, /*index=5*/s32[]{:T(128)}) %tuple.116), condition=%wide.while_cond, body=%wide.while_body.sunk | while | flops 2 | bytes 32913 | solution.py:89
  829.5 44.9 %while.18 = (s32[]{:T(128)}, f32[4,4,2304]{2,1,0:T(4,128)S(1)}, s32[16,3]{0,1:T(4,128)S(1)}, f32[16,2048]{1,0:T(8,128)S(1)}, s32[]{:T(128)}, /*index=5*/s32[]{:T(128)}) while((s32[]{:T(128)}, f32[4,4,2304]{2,1,0:T(4,128)S(1)}, s32[16,3]{0,1:T(4,128)S(1)}, f32[16,2048]{1,0:T(8,128)S(1)}, s32[]{:T(128)}, /*index=5*/s32[]{:T(128)}) %tuple.116), condition=%wide.while_cond, body=%wide.while_body.sunk | while | flops 2 | bytes 32913 | solution.py:89
  886.2 44.9 %while.18 = (s32[]{:T(128)}, f32[4,4,2304]{2,1,0:T(4,128)S(1)}, s32[16,3]{0,1:T(4,128)S(1)}, f32[16,2048]{1,0:T(8,128)S(1)}, s32[]{:T(128)}, /*index=5*/s32[]{:T(128)}) while((s32[]{:T(128)}, f32[4,4,2304]{2,1,0:T(4,128)S(1)}, s32[16,3]{0,1:T(4,128)S(1)}, f32[16,2048]{1,0:T(8,128)S(1)}, s32[]{:T(128)}, /*index=5*/s32[]{:T(128)}) %tuple.116), condition=%wide.while_cond, body=%wide.while_body.sunk | while | flops 2 | bytes 32913 | solution.py:89
  942.9 44.9 %while.18 = (s32[]{:T(128)}, f32[4,4,2304]{2,1,0:T(4,128)S(1)}, s32[16,3]{0,1:T(4,128)S(1)}, f32[16,2048]{1,0:T(8,128)S(1)}, s32[]{:T(128)}, /*index=5*/s32[]{:T(128)}) while((s32[]{:T(128)}, f32[4,4,2304]{2,1,0:T(4,128)S(1)}, s32[16,3]{0,1:T(4,128)S(1)}, f32[16,2048]{1,0:T(8,128)S(1)}, s32[]{:T(128)}, /*index=5*/s32[]{:T(128)}) %tuple.116), condition=%wide.while_cond, body=%wide.while_body.sunk | while | flops 2 | bytes 32913 | solution.py:89
  999.6 44.9 %while.18 = (s32[]{:T(128)}, f32[4,4,2304]{2,1,0:T(4,128)S(1)}, s32[16,3]{0,1:T(4,128)S(1)}, f32[16,2048]{1,0:T(8,128)S(1)}, s32[]{:T(128)}, /*index=5*/s32[]{:T(128)}) while((s32[]{:T(128)}, f32[4,4,2304]{2,1,0:T(4,128)S(1)}, s32[16,3]{0,1:T(4,128)S(1)}, f32[16,2048]{1,0:T(8,128)S(1)}, s32[]{:T(128)}, /*index=5*/s32[]{:T(128)}) %tuple.116), condition=%wide.while_cond, body=%wide.while_body.sunk | while | flops 2 | bytes 32913 | solution.py:89
  1056.3 44.9 %while.18 = (s32[]{:T(128)}, f32[4,4,2304]{2,1,0:T(4,128)S(1)}, s32[16,3]{0,1:T(4,128)S(1)}, f32[16,2048]{1,0:T(8,128)S(1)}, s32[]{:T(128)}, /*index=5*/s32[]{:T(128)}) while((s32[]{:T(128)}, f32[4,4,2304]{2,1,0:T(4,128)S(1)}, s32[16,3]{0,1:T(4,128)S(1)}, f32[16,2048]{1,0:T(8,128)S(1)}, s32[]{:T(128)}, /*index=5*/s32[]{:T(128)}) %tuple.116), condition=%wide.while_cond, body=%wide.while_body.sunk | while | flops 2 | bytes 32913 | solution.py:89
  1113.0 44.9 %while.18 = (s32[]{:T(128)}, f32[4,4,2304]{2,1,0:T(4,128)S(1)}, s32[16,3]{0,1:T(4,128)S(1)}, f32[16,2048]{1,0:T(8,128)S(1)}, s32[]{:T(128)}, /*index=5*/s32[]{:T(128)}) while((s32[]{:T(128)}, f32[4,4,2304]{2,1,0:T(4,128)S(1)}, s32[16,3]{0,1:T(4,128)S(1)}, f32[16,2048]{1,0:T(8,128)S(1)}, s32[]{:T(128)}, /*index=5*/s32[]{:T(128)}) %tuple.116), condition=%wide.while_cond, body=%wide.while_body.sunk | while | flops 2 | bytes 32913 | solution.py:89
  1169.7 44.9 %while.18 = (s32[]{:T(128)}, f32[4,4,2304]{2,1,0:T(4,128)S(1)}, s32[16,3]{0,1:T(4,128)S(1)}, f32[16,2048]{1,0:T(8,128)S(1)}, s32[]{:T(128)}, /*index=5*/s32[]{:T(128)}) while((s32[]{:T(128)}, f32[4,4,2304]{2,1,0:T(4,128)S(1)}, s32[16,3]{0,1:T(4,128)S(1)}, f32[16,2048]{1,0:T(8,128)S(1)}, s32[]{:T(128)}, /*index=5*/s32[]{:T(128)}) %tuple.116), condition=%wide.while_cond, body=%wide.while_body.sunk | while | flops 2 | bytes 32913 | solution.py:89
  1226.4 44.9 %while.18 = (s32[]{:T(128)}, f32[4,4,2304]{2,1,0:T(4,128)S(1)}, s32[16,3]{0,1:T(4,128)S(1)}, f32[16,2048]{1,0:T(8,128)S(1)}, s32[]{:T(128)}, /*index=5*/s32[]{:T(128)}) while((s32[]{:T(128)}, f32[4,4,2304]{2,1,0:T(4,128)S(1)}, s32[16,3]{0,1:T(4,128)S(1)}, f32[16,2048]{1,0:T(8,128)S(1)}, s32[]{:T(128)}, /*index=5*/s32[]{:T(128)}) %tuple.116), condition=%wide.while_cond, body=%wide.while_body.sunk | while | flops 2 | bytes 32913 | solution.py:89
  1283.1 44.9 %while.18 = (s32[]{:T(128)}, f32[4,4,2304]{2,1,0:T(4,128)S(1)}, s32[16,3]{0,1:T(4,128)S(1)}, f32[16,2048]{1,0:T(8,128)S(1)}, s32[]{:T(128)}, /*index=5*/s32[]{:T(128)}) while((s32[]{:T(128)}, f32[4,4,2304]{2,1,0:T(4,128)S(1)}, s32[16,3]{0,1:T(4,128)S(1)}, f32[16,2048]{1,0:T(8,128)S(1)}, s32[]{:T(128)}, /*index=5*/s32[]{:T(128)}) %tuple.116), condition=%wide.while_cond, body=%wide.while_body.sunk | while | flops 2 | bytes 32913 | solution.py:89
  1339.8 44.9 %while.18 = (s32[]{:T(128)}, f32[4,4,2304]{2,1,0:T(4,128)S(1)}, s32[16,3]{0,1:T(4,128)S(1)}, f32[16,2048]{1,0:T(8,128)S(1)}, s32[]{:T(128)}, /*index=5*/s32[]{:T(128)}) while((s32[]{:T(128)}, f32[4,4,2304]{2,1,0:T(4,128)S(1)}, s32[16,3]{0,1:T(4,128)S(1)}, f32[16,2048]{1,0:T(8,128)S(1)}, s32[]{:T(128)}, /*index=5*/s32[]{:T(128)}) %tuple.116), condition=%wide.while_cond, body=%wide.while_body.sunk | while | flops 2 | bytes 32913 | solution.py:89
  1396.5 44.9 %while.18 = (s32[]{:T(128)}, f32[4,4,2304]{2,1,0:T(4,128)S(1)}, s32[16,3]{0,1:T(4,128)S(1)}, f32[16,2048]{1,0:T(8,128)S(1)}, s32[]{:T(128)}, /*index=5*/s32[]{:T(128)}) while((s32[]{:T(128)}, f32[4,4,2304]{2,1,0:T(4,128)S(1)}, s32[16,3]{0,1:T(4,128)S(1)}, f32[16,2048]{1,0:T(8,128)S(1)}, s32[]{:T(128)}, /*index=5*/s32[]{:T(128)}) %tuple.116), condition=%wide.while_cond, body=%wide.while_body.sunk | while | flops 2 | bytes 32913 | solution.py:89
  1453.2 44.9 %while.18 = (s32[]{:T(128)}, f32[4,4,2304]{2,1,0:T(4,128)S(1)}, s32[16,3]{0,1:T(4,128)S(1)}, f32[16,2048]{1,0:T(8,128)S(1)}, s32[]{:T(128)}, /*index=5*/s32[]{:T(128)}) while((s32[]{:T(128)}, f32[4,4,2304]{2,1,0:T(4,128)S(1)}, s32[16,3]{0,1:T(4,128)S(1)}, f32[16,2048]{1,0:T(8,128)S(1)}, s32[]{:T(128)}, /*index=5*/s32[]{:T(128)}) %tuple.116), condition=%wide.while_cond, body=%wide.while_body.sunk | while | flops 2 | bytes 32913 | solution.py:89
  1509.8 44.9 %while.18 = (s32[]{:T(128)}, f32[4,4,2304]{2,1,0:T(4,128)S(1)}, s32[16,3]{0,1:T(4,128)S(1)}, f32[16,2048]{1,0:T(8,128)S(1)}, s32[]{:T(128)}, /*index=5*/s32[]{:T(128)}) while((s32[]{:T(128)}, f32[4,4,2304]{2,1,0:T(4,128)S(1)}, s32[16,3]{0,1:T(4,128)S(1)}, f32[16,2048]{1,0:T(8,128)S(1)}, s32[]{:T(128)}, /*index=5*/s32[]{:T(128)}) %tuple.116), condition=%wide.while_cond, body=%wide.while_body.sunk | while | flops 2 | bytes 32913 | solution.py:89
  1566.5 44.9 %while.18 = (s32[]{:T(128)}, f32[4,4,2304]{2,1,0:T(4,128)S(1)}, s32[16,3]{0,1:T(4,128)S(1)}, f32[16,2048]{1,0:T(8,128)S(1)}, s32[]{:T(128)}, /*index=5*/s32[]{:T(128)}) while((s32[]{:T(128)}, f32[4,4,2304]{2,1,0:T(4,128)S(1)}, s32[16,3]{0,1:T(4,128)S(1)}, f32[16,2048]{1,0:T(8,128)S(1)}, s32[]{:T(128)}, /*index=5*/s32[]{:T(128)}) %tuple.116), condition=%wide.while_cond, body=%wide.while_body.sunk | while | flops 2 | bytes 32913 | solution.py:89
  1623.2 44.9 %while.18 = (s32[]{:T(128)}, f32[4,4,2304]{2,1,0:T(4,128)S(1)}, s32[16,3]{0,1:T(4,128)S(1)}, f32[16,2048]{1,0:T(8,128)S(1)}, s32[]{:T(128)}, /*index=5*/s32[]{:T(128)}) while((s32[]{:T(128)}, f32[4,4,2304]{2,1,0:T(4,128)S(1)}, s32[16,3]{0,1:T(4,128)S(1)}, f32[16,2048]{1,0:T(8,128)S(1)}, s32[]{:T(128)}, /*index=5*/s32[]{:T(128)}) %tuple.116), condition=%wide.while_cond, body=%wide.while_body.sunk | while | flops 2 | bytes 32913 | solution.py:89
  1668.3 39.7 %psum.39 = f32[4,2048]{1,0:T(4,128)S(1)} all-reduce(f32[4,2048]{1,0:T(4,128)S(1)} %get-tuple-element.70), channel_id=1, replica_groups=mesh['tm'=64,'sta'=4] {'sta'}, use_global_device_ids=true, to_apply=%region_15.16 | all-reduce | flops 8192 | bytes 65536 | tf_op jit(solution)/shard_map/psum | solution.py:95
  1708.1 153.4 %pmax.7 = f32[4]{0:T(128)S(1)} all-reduce(f32[4]{0:T(128)S(1)} %abs_reduce_fusion), channel_id=1, replica_groups=mesh['tm'=64,'sta'=4] {'tm'}, use_global_device_ids=true, to_apply=%region_17.18 | all-reduce | flops 4 | bytes 32 | tf_op jit(solution)/shard_map/pmax | solution.py:96
  (2447 shorter events, 1015.9 us)
Async XLA Ops:
  6.5 8.2 copy-start.6
  6.5 8.1 copy-start.7
  6.5 635.3 %all-reduce.7.cloned.1.call-start = ((), (), s32[]{:S(2)}) async-start(), calls=%async_computation | async-start | bytes 1179648 | tf_op jit(solution)/shard_map/psum | solution.py:21
  7.5 7.2 collective-permute-start
  641.9 4.0 copy-start.2
  641.9 4.0 copy-start.3
  659.1 45.4 %copy-start.5 = (bf16[18,4,3328]{2,1,0:T(4,128)(2,1)S(1)}, bf16[18,4,3328]{2,1,0:T(4,128)(2,1)}, u32[]{:S(2)}) copy-start(bf16[18,4,3328]{2,1,0:T(4,128)(2,1)} %copy-done.4) | copy-start | bytes 1437700 | tf_op jit(solution)/shard_map/while
  715.8 45.4 %copy-start.5 = (bf16[18,4,3328]{2,1,0:T(4,128)(2,1)S(1)}, bf16[18,4,3328]{2,1,0:T(4,128)(2,1)}, u32[]{:S(2)}) copy-start(bf16[18,4,3328]{2,1,0:T(4,128)(2,1)} %copy-done.4) | copy-start | bytes 1437700 | tf_op jit(solution)/shard_map/while
  772.5 45.4 %copy-start.5 = (bf16[18,4,3328]{2,1,0:T(4,128)(2,1)S(1)}, bf16[18,4,3328]{2,1,0:T(4,128)(2,1)}, u32[]{:S(2)}) copy-start(bf16[18,4,3328]{2,1,0:T(4,128)(2,1)} %copy-done.4) | copy-start | bytes 1437700 | tf_op jit(solution)/shard_map/while
  829.2 45.4 %copy-start.5 = (bf16[18,4,3328]{2,1,0:T(4,128)(2,1)S(1)}, bf16[18,4,3328]{2,1,0:T(4,128)(2,1)}, u32[]{:S(2)}) copy-start(bf16[18,4,3328]{2,1,0:T(4,128)(2,1)} %copy-done.4) | copy-start | bytes 1437700 | tf_op jit(solution)/shard_map/while
  885.9 45.4 %copy-start.5 = (bf16[18,4,3328]{2,1,0:T(4,128)(2,1)S(1)}, bf16[18,4,3328]{2,1,0:T(4,128)(2,1)}, u32[]{:S(2)}) copy-start(bf16[18,4,3328]{2,1,0:T(4,128)(2,1)} %copy-done.4) | copy-start | bytes 1437700 | tf_op jit(solution)/shard_map/while
  942.6 45.4 %copy-start.5 = (bf16[18,4,3328]{2,1,0:T(4,128)(2,1)S(1)}, bf16[18,4,3328]{2,1,0:T(4,128)(2,1)}, u32[]{:S(2)}) copy-start(bf16[18,4,3328]{2,1,0:T(4,128)(2,1)} %copy-done.4) | copy-start | bytes 1437700 | tf_op jit(solution)/shard_map/while
  999.3 45.4 %copy-start.5 = (bf16[18,4,3328]{2,1,0:T(4,128)(2,1)S(1)}, bf16[18,4,3328]{2,1,0:T(4,128)(2,1)}, u32[]{:S(2)}) copy-start(bf16[18,4,3328]{2,1,0:T(4,128)(2,1)} %copy-done.4) | copy-start | bytes 1437700 | tf_op jit(solution)/shard_map/while
  1056.0 45.4 %copy-start.5 = (bf16[18,4,3328]{2,1,0:T(4,128)(2,1)S(1)}, bf16[18,4,3328]{2,1,0:T(4,128)(2,1)}, u32[]{:S(2)}) copy-start(bf16[18,4,3328]{2,1,0:T(4,128)(2,1)} %copy-done.4) | copy-start | bytes 1437700 | tf_op jit(solution)/shard_map/while
  1112.7 45.4 %copy-start.5 = (bf16[18,4,3328]{2,1,0:T(4,128)(2,1)S(1)}, bf16[18,4,3328]{2,1,0:T(4,128)(2,1)}, u32[]{:S(2)}) copy-start(bf16[18,4,3328]{2,1,0:T(4,128)(2,1)} %copy-done.4) | copy-start | bytes 1437700 | tf_op jit(solution)/shard_map/while
  1169.4 45.4 %copy-start.5 = (bf16[18,4,3328]{2,1,0:T(4,128)(2,1)S(1)}, bf16[18,4,3328]{2,1,0:T(4,128)(2,1)}, u32[]{:S(2)}) copy-start(bf16[18,4,3328]{2,1,0:T(4,128)(2,1)} %copy-done.4) | copy-start | bytes 1437700 | tf_op jit(solution)/shard_map/while
  1226.1 45.4 %copy-start.5 = (bf16[18,4,3328]{2,1,0:T(4,128)(2,1)S(1)}, bf16[18,4,3328]{2,1,0:T(4,128)(2,1)}, u32[]{:S(2)}) copy-start(bf16[18,4,3328]{2,1,0:T(4,128)(2,1)} %copy-done.4) | copy-start | bytes 1437700 | tf_op jit(solution)/shard_map/while
  1282.8 45.4 %copy-start.5 = (bf16[18,4,3328]{2,1,0:T(4,128)(2,1)S(1)}, bf16[18,4,3328]{2,1,0:T(4,128)(2,1)}, u32[]{:S(2)}) copy-start(bf16[18,4,3328]{2,1,0:T(4,128)(2,1)} %copy-done.4) | copy-start | bytes 1437700 | tf_op jit(solution)/shard_map/while
  1339.5 45.4 %copy-start.5 = (bf16[18,4,3328]{2,1,0:T(4,128)(2,1)S(1)}, bf16[18,4,3328]{2,1,0:T(4,128)(2,1)}, u32[]{:S(2)}) copy-start(bf16[18,4,3328]{2,1,0:T(4,128)(2,1)} %copy-done.4) | copy-start | bytes 1437700 | tf_op jit(solution)/shard_map/while
  1396.2 45.4 %copy-start.5 = (bf16[18,4,3328]{2,1,0:T(4,128)(2,1)S(1)}, bf16[18,4,3328]{2,1,0:T(4,128)(2,1)}, u32[]{:S(2)}) copy-start(bf16[18,4,3328]{2,1,0:T(4,128)(2,1)} %copy-done.4) | copy-start | bytes 1437700 | tf_op jit(solution)/shard_map/while
  1452.8 45.4 %copy-start.5 = (bf16[18,4,3328]{2,1,0:T(4,128)(2,1)S(1)}, bf16[18,4,3328]{2,1,0:T(4,128)(2,1)}, u32[]{:S(2)}) copy-start(bf16[18,4,3328]{2,1,0:T(4,128)(2,1)} %copy-done.4) | copy-start | bytes 1437700 | tf_op jit(solution)/shard_map/while
  1509.5 45.4 %copy-start.5 = (bf16[18,4,3328]{2,1,0:T(4,128)(2,1)S(1)}, bf16[18,4,3328]{2,1,0:T(4,128)(2,1)}, u32[]{:S(2)}) copy-start(bf16[18,4,3328]{2,1,0:T(4,128)(2,1)} %copy-done.4) | copy-start | bytes 1437700 | tf_op jit(solution)/shard_map/while
  1566.2 45.4 %copy-start.5 = (bf16[18,4,3328]{2,1,0:T(4,128)(2,1)S(1)}, bf16[18,4,3328]{2,1,0:T(4,128)(2,1)}, u32[]{:S(2)}) copy-start(bf16[18,4,3328]{2,1,0:T(4,128)(2,1)} %copy-done.4) | copy-start | bytes 1437700 | tf_op jit(solution)/shard_map/while
  1622.9 45.4 %copy-start.5 = (bf16[18,4,3328]{2,1,0:T(4,128)(2,1)S(1)}, bf16[18,4,3328]{2,1,0:T(4,128)(2,1)}, u32[]{:S(2)}) copy-start(bf16[18,4,3328]{2,1,0:T(4,128)(2,1)} %copy-done.4) | copy-start | bytes 1437700 | tf_op jit(solution)/shard_map/while
  (20 other events, 21.9 us)
Sparse Core Ops, SparseCore 0:
  14.8 627.0 all-reduce.6
where the time goes:
time: 1910 us; the launch traced here: 1870 us
  local copies, waits for them, and re-layouts  952 us (50%)
  waiting for transfers between devices  627 us (33%)
  blocking collectives  193 us (10%)
  other arithmetic  58 us (3%)
    gather x1152, local copies, waits for them, and re-layouts  800 us
    psum x1, waiting for transfers between devices, broadcast(): return lax.psum(block, axis)  627 us
    pmax x1, blocking collectives, on_device(): peaks = lax.pmax(jnp.max(jnp.abs(summed), axis=1), 'tm')  153 us
    while x684, local copies, waits for them, and re-layouts  67.9 us
    psum x1, blocking collectives, on_device(): summed = lax.psum(partial_stack, 'sta')  39.7 us
  transfers between devices with their start and end apart: 2, of which 1 were waited for; matrix products, arithmetic and copies ran while one was open for 0% of the time, Pallas kernels for 0%

commit v1 on v0

v1 whole, which is shorter than its diff:
```python
import jax
import jax.numpy as jnp
from jax import lax
from jax.experimental import pallas as pl
from jax.experimental.pallas import tpu as pltpu
from jax.sharding import PartitionSpec as P

TL = 1024
B = 128
GROUP = 8
PIECE = 16
OUT_ROWS = GROUP * PIECE
ROWS = OUT_ROWS + 8
ALL_ROWS = ROWS + 8
LAGS = TL // B + 1
K = 4
MESH = pl.DeviceIdType.MESH
f32, bf16 = jnp.float32, jnp.bfloat16


def place():
    me = lax.axis_index("tm")
    z = lax.div(me, GROUP)
    return z, me - z * GROUP, lax.axis_size("tm") // GROUP


def others(mine, count, shift=1):
    return [lax.rem(mine + shift * i + count, count) for i in range(1, count)]


def greet(devices):
    barrier = pltpu.get_barrier_semaphore()
    for device in devices:
        pl.semaphore_signal(barrier, inc=1, device_id=device, device_id_type=MESH)
    pl.semaphore_wait(barrier, len(devices))


def remote(src, dst, send_sem, recv_sem, device):
    return pltpu.make_async_remote_copy(
        src_ref=src, dst_ref=dst, send_sem=send_sem, recv_sem=recv_sem, device_id=device, device_id_type=MESH
    )


def fetch_kernel(select_ref, data_ref, bank_ref, rows_ref, tpl_ref, raw, part, got, sems, own_sems):
    z, p, depth = place()
    per = data_ref.shape[0] // GROUP
    in_group = lambda q: {"tm": z * GROUP + q}
    in_depth = lambda w: {"tm": w * GROUP + p}
    greet([in_group(q) for q in others(p, GROUP)] + [in_depth(w) for w in others(z, depth)])

    own_data = pltpu.make_async_copy(data_ref.at[pl.ds(p * per, per)], rows_ref.at[p], own_sems.at[0])
    own_bank = pltpu.make_async_copy(bank_ref.at[pl.ds(p * per, per)], raw.at[p], own_sems.at[1])
    own_bank.start()
    own_data.start()

    def bank_copy(owner, q):
        return remote(bank_ref.at[pl.ds(q * per, per)], raw.at[owner], sems.at[0, q], sems.at[1, owner], in_group(q))

    def data_copy(owner, q):
        return remote(data_ref.at[pl.ds(q * per, per)], rows_ref.at[owner], sems.at[2, q], sems.at[3, owner], in_group(q))

    def part_copy(owner, w):
        return remote(part.at[w], got.at[owner], sems.at[4, w], sems.at[5, owner], in_depth(w))

    def tpl_copy(owner, w):
        return remote(tpl_ref.at[owner], tpl_ref.at[owner], sems.at[6, w], sems.at[7, owner], in_depth(w))

    for q in others(p, GROUP):
        bank_copy(p, q).start()
    for q in others(p, GROUP):
        data_copy(p, q).start()

    own_bank.wait()
    for q in others(p, GROUP, -1):
        bank_copy(q, p).wait_recv()
    for k in range(K):
        wanted = select_ref[k] - z * GROUP
        picked = jnp.zeros(raw.shape[1:], f32)
        for j in range(GROUP):
            picked += jnp.where(wanted == j, raw[j].astype(f32), 0.0)
        picked = picked.astype(bf16)
        for half in range(2):
            part[2 * k + half] = picked[4 * half : 4 * half + 5]
    for w in others(z, depth):
        part_copy(z, w).start()
    got[z] = part[z]

    own_data.wait()
    for q in others(p, GROUP, -1):
        data_copy(q, p).wait_recv()
    before, after = lax.rem(z + depth - 1, depth), lax.rem(z + 1, depth)
    halo = remote(rows_ref.at[0], rows_ref.at[GROUP], own_sems.at[2], own_sems.at[3], in_depth(before))
    halo.start()

    for w in others(z, depth, -1):
        part_copy(w, z).wait_recv()
    tpl = got[0].astype(f32)
    for j in range(1, GROUP):
        tpl += got[j].astype(f32)
    mean = jnp.sum(jnp.sum(tpl, axis=2, keepdims=True), axis=1, keepdims=True) / TL
    centred = tpl - mean
    power = jnp.sum(jnp.sum(centred * centred, axis=2, keepdims=True), axis=1, keepdims=True)
    normed = (centred * lax.rsqrt(power + 1e-05)).astype(bf16)
    tpl_ref[z] = normed
    for w in others(z, depth):
        tpl_copy(z, w).start()
    for w in others(z, depth, -1):
        tpl_copy(w, z).wait_recv()
    halo.wait()
    for q in others(p, GROUP):
        bank_copy(p, q).wait_send()
        data_copy(p, q).wait_send()
    for w in others(z, depth):
        part_copy(z, w).wait_send()
        tpl_copy(z, w).wait_send()


def fetch(select, data, bank):
    per = data.shape[0] // GROUP
    vmem = pl.BlockSpec(memory_space=pltpu.VMEM)
    return pl.pallas_call(
        fetch_kernel,
        out_shape=[
            jax.ShapeDtypeStruct((GROUP + 1, per, PIECE, B), bf16),
            jax.ShapeDtypeStruct((2 * K, 5, TL // B, B), bf16),
        ],
        in_specs=[pl.BlockSpec(memory_space=pltpu.SMEM), vmem, vmem],
        out_specs=[vmem, vmem],
        scratch_shapes=[
            pltpu.VMEM((GROUP, per, TL // B, B), bf16),
            pltpu.VMEM((2 * K, 5, TL // B, B), bf16),
            pltpu.VMEM((2 * K, 5, TL // B, B), bf16),
            pltpu.SemaphoreType.DMA((8, GROUP)),
            pltpu.SemaphoreType.DMA((4,)),
        ],
        compiler_params=pltpu.CompilerParams(
            collective_id=0, has_side_effects=True, vmem_limit_bytes=16 * 2**20
        ),
    )(select, data, bank)


def correlate_kernel(rows_ref, tpl_ref, shifts_ref, out_ref, x_ref, toeplitz, moved):
    z, p, depth = place()
    per = rows_ref.shape[1]
    row = lax.broadcasted_iota(jnp.int32, (ALL_ROWS, B), 0)
    lane = lax.broadcasted_iota(jnp.int32, (OUT_ROWS, B), 1)
    before = lax.broadcasted_iota(jnp.int32, (B, 2 * B), 0) < lax.broadcasted_iota(jnp.int32, (B, 2 * B), 1)
    sums = jnp.where(before, 1.0, 0.0).astype(bf16)
    flip_at = lax.broadcasted_iota(jnp.int32, (B, B), 0) + lax.broadcasted_iota(jnp.int32, (B, B), 1)
    flip = jnp.where(flip_at == B - 1, 1.0, 0.0).astype(bf16)
    valid = jnp.where(z == depth - 1, OUT_ROWS, ALL_ROWS)
    out_ref[...] = jnp.zeros_like(out_ref)

    def dot(a, b):
        return jnp.dot(a, b, preferred_element_type=f32)

    def windows(v):
        ahead, total = v[:, :B], v[:, B:]
        two = total[0:143] + total[1:144]
        four = two[0:141] + two[2:143]
        eight = four[0:136] + four[4:140]
        return eight - ahead[0:136] + ahead[8:144]

    def channel(c, carry):
        x = jnp.where(row < valid, rows_ref[:, c].astype(f32).reshape(ALL_ROWS, B), 0.0)
        x_ref[...] = x
        square = x * x
        high = square.astype(bf16)
        low = (square - high.astype(f32)).astype(bf16)
        window_sum = windows(dot(x.astype(bf16), sums))
        window_sq = windows(dot(high, sums) + dot(low, sums))
        scale = lax.rsqrt(jnp.maximum(window_sq - window_sum * window_sum / TL, TL / 8.0))
        half = lax.div(c, 5)
        zero = jnp.zeros((1, B), f32)
        for k in range(K):
            tpl = dot(tpl_ref[2 * k + half, c - 4 * half], flip)
            line = jnp.concatenate([zero] + [tpl[7 - m : 8 - m] for m in range(TL // B)] + [zero], axis=1)
            for g in range(0, B, 16):
                wide = jnp.broadcast_to(line, (16, line.shape[1]))
                rolled = pltpu.roll(wide, 1 + g, axis=1, stride=1, stride_axis=0).astype(bf16)
                for b in range(LAGS):
                    toeplitz[b * B + g : b * B + g + 16, k * B : (k + 1) * B] = rolled[:, (9 - b) * B : (10 - b) * B]
        series = jnp.concatenate([x_ref[b : b + ROWS] for b in range(LAGS)], axis=1).astype(bf16)
        correl = dot(series, toeplitz[...])
        for k in range(K):
            shift = shifts_ref[k, p * per + c]
            whole = lax.div(shift, B)
            rest = shift - whole * B
            moved[k] = pltpu.roll(correl[:, k * B : (k + 1) * B] * scale, lax.rem(B - rest, B), axis=1)
            here, there = moved[k, pl.ds(whole, OUT_ROWS)], moved[k, pl.ds(whole + 1, OUT_ROWS)]
            out_ref[:, k] += jnp.where(lane < B - rest, here, there).reshape(GROUP, PIECE, B)
        return carry

    lax.fori_loop(0, per, channel, 0)


def correlate(rows, tpl, shifts):
    vmem = pl.BlockSpec(memory_space=pltpu.VMEM)
    return pl.pallas_call(
        correlate_kernel,
        out_shape=jax.ShapeDtypeStruct((GROUP, K, PIECE, B), f32),
        in_specs=[vmem, vmem, pl.BlockSpec(memory_space=pltpu.SMEM)],
        out_specs=vmem,
        scratch_shapes=[
            pltpu.VMEM((ALL_ROWS, B), f32),
            pltpu.VMEM((LAGS * B, K * B), bf16),
            pltpu.VMEM((K, ROWS, B), f32),
        ],
        compiler_params=pltpu.CompilerParams(vmem_limit_bytes=32 * 2**20),
    )(rows, tpl, shifts)


def finish_kernel(stack_ref, out_ref, from_group, from_sta, mine, peaks, sems):
    z, p, depth = place()
    s = lax.axis_index("sta")
    in_group = lambda q: {"tm": z * GROUP + q}
    in_depth = lambda w: {"tm": w * GROUP + p}
    in_sta = lambda t: {"sta": t}
    greet(
        [in_group(q) for q in others(p, GROUP)]
        + [in_depth(w) for w in others(z, depth)]
        + [in_sta(t) for t in others(s, K)]
    )

    def stack_copy(owner, q):
        return remote(stack_ref.at[q], from_group.at[owner], sems.at[0, q], sems.at[1, owner], in_group(q))

    def sta_copy(owner, t):
        return remote(mine.at[t], from_sta.at[owner], sems.at[2, t], sems.at[3, owner], in_sta(t))

    def peak_copy(owner, q):
        return remote(peaks.at[0, p], peaks.at[0, owner], sems.at[4, q], sems.at[5, owner], in_group(q))

    def top_copy(owner, w):
        return remote(peaks.at[1, z], peaks.at[1, owner], sems.at[6, w], sems.at[7, owner], in_depth(w))

    for q in others(p, GROUP):
        stack_copy(p, q).start()
    from_group[p] = stack_ref[p]
    for q in others(p, GROUP, -1):
        stack_copy(q, p).wait_recv()
    total = from_group[0]
    for j in range(1, GROUP):
        total += from_group[j]
    mine[...] = total
    for t in others(s, K):
        sta_copy(s, t).start()
    from_sta[s] = mine[s]
    for t in others(s, K, -1):
        sta_copy(t, s).wait_recv()
    stack = from_sta[0]
    for j in range(1, K):
        stack += from_sta[j]
    size = jnp.abs(stack)
    peaks[0, p] = jnp.maximum(size[:8], size[8:])
    for q in others(p, GROUP):
        peak_copy(p, q).start()
    for q in others(p, GROUP, -1):
        peak_copy(q, p).wait_recv()
    peaks[1, z] = jnp.max(peaks[0], axis=0)
    for w in others(z, depth):
        top_copy(z, w).start()
    for w in others(z, depth, -1):
        top_copy(w, z).wait_recv()
    peak = jnp.max(peaks[1])
    out_ref[...] = stack / (peak + 1e-06)
    for q in others(p, GROUP):
        stack_copy(p, q).wait_send()
        peak_copy(p, q).wait_send()
    for t in others(s, K):
        sta_copy(s, t).wait_send()
    for w in others(z, depth):
        top_copy(z, w).wait_send()


def finish(stack):
    vmem = pl.BlockSpec(memory_space=pltpu.VMEM)
    return pl.pallas_call(
        finish_kernel,
        out_shape=jax.ShapeDtypeStruct((PIECE, B), f32),
        in_specs=[vmem],
        out_specs=vmem,
        scratch_shapes=[
            pltpu.VMEM((GROUP, K, PIECE, B), f32),
            pltpu.VMEM((K, PIECE, B), f32),
            pltpu.VMEM((K, PIECE, B), f32),
            pltpu.VMEM((2, GROUP, 8, B), f32),
            pltpu.SemaphoreType.DMA((8, GROUP)),
        ],
        compiler_params=pltpu.CompilerParams(
            collective_id=1, has_side_effects=True, vmem_limit_bytes=16 * 2**20
        ),
    )(stack)


def on_device(data, bank, select, shifts):
    channels = data.shape[0]
    rows, tpl = fetch(select, data.reshape(channels, PIECE, B), bank.reshape(channels, TL // B, B))
    stack = correlate(rows, tpl, shifts)
    return finish(stack).reshape(1, PIECE * B)


def solution(mesh):
    in_specs = (P("sta", "tm"), P("tm", "sta", None), P(), P(None, "sta"))
    out_specs = P("sta", "tm")
    return jax.shard_map(on_device, mesh=mesh, in_specs=in_specs, out_specs=out_specs, check_vma=False)
```

time: 1910 us -> 62.6 us (0.03); the launches traced: 1870 us -> 62.4 us
  local copies, waits for them, and re-layouts: 952 us -> 3 us
  waiting for transfers between devices: 627 us -> 0 us
  blocking collectives: 193 us -> 0 us
  Pallas kernels: 0 us -> 59.4 us
  other arithmetic: 58 us -> 0 us
    gather x1188 -> x0, local copies, waits for them, and re-layouts: 802 us -> none
    psum x1 -> x0, waiting for transfers between devices: 627 us -> none  [broadcast(): return lax.psum(block, axis)]
    pmax x1 -> x0, blocking collectives: 153 us -> none  [on_device(): peaks = lax.pmax(jnp.max(jnp.abs(summed), axis=1), 'tm')]
    while x684 -> x0, local copies, waits for them, and re-layouts: 67.9 us -> none
    pallas_call x0 -> x3, Pallas kernels: none -> 59.4 us  [the longest x1 25.6 us: fetch(): pl.pallas_call(fetch_kernel, out_shape=[jax.ShapeDtypeStruct((GROUP + 1,...]
    another operation x72 -> x0, other arithmetic: 42.1 us -> none  [the longest x36 31.9 us: window_sums(): inner_sums = jnp.cumsum(blocks, axis=-1) - blocks]
    psum x1 -> x0, blocking collectives: 39.7 us -> none  [on_device(): summed = lax.psum(partial_stack, 'sta')]
    concatenate x18 -> x0, local copies, waits for them, and re-layouts: 32.9 us -> none  [group_step(): jnp.concatenate([blocked[:, q:q + starts, :] for q in range(lag_padded)],...]
  transfers between devices with their start and end apart: 2 -> 0, of which waited for: 1 -> 0; matrix products, arithmetic and copies ran while one was open for 0% -> 0% of each run, Pallas kernels for 0% -> 0%
where the time goes in v1:
time: 62.6 us; the launch traced here: 62.4 us
  Pallas kernels  59.4 us (95%)
  local copies, waits for them, and re-layouts  3 us (5%)
    pallas_call x1, Pallas kernels, fetch(): pl.pallas_call(fetch_kernel, out_shape=[jax.ShapeDtypeStruct((GROUP + 1,...  25.6 us
    pallas_call x1, Pallas kernels, finish(): pl.pallas_call(finish_kernel, out_shape=jax.ShapeDtypeStruct((PIECE, B),...  24.5 us
    pallas_call x1, Pallas kernels, correlate(): pl.pallas_call(correlate_kernel, out_shape=jax.ShapeDtypeStruct((GROUP, K...  9.22 us
    unnamed x9, local copies, waits for them, and re-layouts  3 us

profile of v1, /device:TPU:1, one launch (start us, length us, event | category | flops | bytes accessed | tf_op | source)
XLA Modules:
  0.0 62.4 jit_solution(7487594565722148969)
XLA Ops:
  0.0 0.0 copy-start.2
  0.0 1.0 %copy.6 = bf16[9,8,8,128]{3,2,1,0:T(8,128)(2,1)S(1)} copy(bf16[9,8,8,128]{3,1,2,0:T(8,128)(2,1)} %bitcast.10) | data formatting | bytes 294912
  1.0 0.0 copy-done.2
  1.1 0.0 copy-start.1
  1.1 0.6 %copy-done.1 = s32[4]{0:T(128)S(1)} copy-done((s32[4]{0:T(128)S(1)}, s32[4]{0:T(128)}, u32[]{:S(2)}) %copy-start.1) | copy-done | bytes 40
  1.7 25.6 %shard_map.46 = (bf16[9,9,16,128]{3,2,1,0:T(8,128)(2,1)S(1)}, bf16[8,5,8,128]{3,2,1,0:T(8,128)(2,1)S(1)}) custom-call(s32[4]{0:T(128)S(1)} %copy-done.1, bf16[72,16,128]{2,1,0:T(8,128)(2,1)S(1)} %bitcast.6, bf16[72,8,128]{2,1,0:T(8,128)(2,1)S(1)} %bitcast.7), custom_call_target="tpu_custom_call" | custom-call | tf_op jit(solution)/shard_map/pallas_call | solution.py:121
  27.4 0.0 copy-start
  27.4 0.7 %copy-done = s32[4,72]{1,0:T(4,128)S(1)} copy-done((s32[4,72]{1,0:T(4,128)S(1)}, s32[4,72]{1,0:T(4,128)}, u32[]{:S(2)}) %copy-start) | copy-done | bytes 1176
  28.1 9.2 %shard_map.47.stack_ref = f32[8,4,16,128]{3,2,1,0:T(8,128)S(1)} custom-call(bf16[9,9,16,128]{3,2,1,0:T(8,128)(2,1)S(1)} %get-tuple-element.7.rows_ref, bf16[8,5,8,128]{3,2,1,0:T(8,128)(2,1)S(1)} %get-tuple-element.8.tpl_ref, s32[4,72]{1,0:T(4,128)S(1)} %copy-done), custom_call_target="tpu_custom_call" | custom-call | tf_op jit(solution)/shard_map/pallas_call | solution.py:199
  37.3 24.5 %shard_map.48 = f32[16,128]{1,0:T(8,128)S(1)} custom-call(f32[8,4,16,128]{3,2,1,0:T(8,128)S(1)} %shard_map.47.stack_ref), custom_call_target="tpu_custom_call" | custom-call | tf_op jit(solution)/shard_map/pallas_call | solution.py:278
  61.8 0.6 copy.8
  (1 shorter events, 0.0 us)
Async XLA Ops:
  0.0 1.0 %copy-start.2 = (bf16[72,2048]{1,0:T(8,128)(2,1)S(1)}, bf16[72,2048]{1,0:T(8,128)(2,1)}, u32[]{:S(2)}) copy-start(bf16[72,2048]{1,0:T(8,128)(2,1)} %param.4) | copy-start | bytes 884740
  1.1 0.7 %copy-start.1 = (s32[4]{0:T(128)S(1)}, s32[4]{0:T(128)}, u32[]{:S(2)}) copy-start(s32[4]{0:T(128)} %select_ref.1) | copy-start | bytes 52
  27.4 0.7 %copy-start = (s32[4,72]{1,0:T(4,128)S(1)}, s32[4,72]{1,0:T(4,128)}, u32[]{:S(2)}) copy-start(s32[4,72]{1,0:T(4,128)} %shifts_ref.1) | copy-start | bytes 3460

commit v2 on v0

v2 whole, which is shorter than its diff:
```python
import jax
import jax.numpy as jnp
from jax import lax
from jax.experimental import pallas as pl
from jax.experimental.pallas import tpu as pltpu
from jax.sharding import PartitionSpec as P

TL = 1024
B = 128
TPL_ROWS = TL // B
GROUP = 8
PIECE = 16
OUT_ROWS = GROUP * PIECE
ROWS = OUT_ROWS + 8
ALL_ROWS = ROWS + 8
LAGS = TPL_ROWS + 1
K = 4
MESH = pl.DeviceIdType.MESH
f32, bf16 = jnp.float32, jnp.bfloat16


def dot(a, b):
    return jnp.dot(a, b, preferred_element_type=f32)


def remote(src, dst, sems, device):
    return pltpu.make_async_remote_copy(
        src_ref=src, dst_ref=dst, send_sem=sems.at[0], recv_sem=sems.at[1], device_id=device, device_id_type=MESH
    )


def windows(v):
    ahead, total = v[:, :B], v[:, B:]
    two = total[0:143] + total[1:144]
    four = two[0:141] + two[2:143]
    eight = four[0:136] + four[4:140]
    return eight - ahead[0:136] + ahead[8:144]


def kernel(
    select_hbm, data_hbm, bank_hbm, shifts_hbm, out_ref,
    select_ref, shifts_ref, data_in, bank_in, lay, data_ref, bank_ref, rows_ref, raw, part, got, tpl_ref,
    x_ref, scales, series, toeplitz, moved, stack, from_all, peaks,
    local_sems, bank_sems, data_sems, part_sems, halo_sems, tpl_sems, stack_sems, peak_sems,
):
    me, s = lax.axis_index("tm"), lax.axis_index("sta")
    count = lax.axis_size("tm")
    depth = count // GROUP
    z = lax.div(me, GROUP)
    p = me - z * GROUP
    per = rows_ref.shape[1]
    self = {"tm": me, "sta": s}
    group = [lax.rem(p + i, GROUP) for i in range(1, GROUP)]
    along = [lax.rem(z + i, depth) for i in range(1, depth)]
    in_group = lambda q: {"tm": z * GROUP + q, "sta": s}
    in_depth = lambda w: {"tm": w * GROUP + p, "sta": s}

    barrier = pltpu.get_barrier_semaphore()
    greeted = [in_group(q) for q in group] + [in_depth(w) for w in along]
    greeted += [{"tm": me, "sta": lax.rem(s + i, K)} for i in range(1, K)]
    for device in greeted:
        pl.semaphore_signal(barrier, inc=1, device_id=device, device_id_type=MESH)

    inputs = [(bank_hbm.at[0], bank_in), (data_hbm, data_in), (select_hbm, select_ref), (shifts_hbm, shifts_ref)]
    loads = [pltpu.make_async_copy(src, dst, local_sems.at[i]) for i, (src, dst) in enumerate(inputs)]
    for load in loads:
        load.start()
    channels = data_in.shape[0]
    loads[0].wait()
    for b in range(TPL_ROWS):
        lay[pl.ds(b, channels, stride=TPL_ROWS), :] = bank_in[:, b * B : (b + 1) * B].astype(f32)
    bank_ref[...] = lay[: channels * TPL_ROWS].astype(bf16).reshape(bank_ref.shape)
    loads[1].wait()
    for a in range(PIECE):
        lay[pl.ds(a, channels, stride=PIECE), :] = data_in[:, a * B : (a + 1) * B].astype(f32)
    data_ref[...] = lay[...].astype(bf16).reshape(data_ref.shape)
    loads[2].wait()
    loads[3].wait()
    pl.semaphore_wait(barrier, len(greeted))

    for q in group:
        remote(bank_ref.at[pl.ds(q * per, per)], raw.at[p], bank_sems, in_group(q)).start()
    for q in group:
        remote(data_ref.at[pl.ds(q * per, per)], rows_ref.at[p], data_sems, in_group(q)).start()
    raw[p] = bank_ref[pl.ds(p * per, per)]
    rows_ref[p] = data_ref[pl.ds(p * per, per)]

    bank_all = remote(raw.at[pl.ds(0, GROUP - 1)], raw.at[pl.ds(0, GROUP - 1)], bank_sems, self)
    bank_all.wait_recv()
    for k in range(K):
        wanted = select_ref[k] - z * GROUP
        picked = jnp.zeros(raw.shape[1:], f32)
        for j in range(GROUP):
            picked += jnp.where(wanted == j, raw[j].astype(f32), 0.0)
        picked = picked.astype(bf16)
        for half in range(2):
            part[2 * k + half] = picked[4 * half : 4 * half + 5]
    for w in along:
        remote(part.at[w], got.at[z], part_sems, in_depth(w)).start()
    got[z] = part[z]

    data_all = remote(rows_ref.at[pl.ds(0, GROUP - 1)], rows_ref.at[pl.ds(0, GROUP - 1)], data_sems, self)
    data_all.wait_recv()
    halo = remote(rows_ref.at[0], rows_ref.at[GROUP], halo_sems, in_depth(lax.rem(z + depth - 1, depth)))
    halo.start()

    part_all = remote(got.at[pl.ds(0, depth - 1)], got.at[pl.ds(0, depth - 1)], part_sems, self)
    part_all.wait_recv()
    tpl = got[0].astype(f32)
    for j in range(1, GROUP):
        tpl += got[j].astype(f32)
    mean = jnp.sum(jnp.sum(tpl, axis=2, keepdims=True), axis=1, keepdims=True) / TL
    centred = tpl - mean
    power = jnp.sum(jnp.sum(centred * centred, axis=2, keepdims=True), axis=1, keepdims=True)
    tpl_ref[z] = (centred * lax.rsqrt(power + 1e-05)).astype(bf16)
    for w in along:
        remote(tpl_ref.at[z], tpl_ref.at[z], tpl_sems, in_depth(w)).start()

    halo.wait_recv()
    row = lax.broadcasted_iota(jnp.int32, (ALL_ROWS, B), 0)
    before = lax.broadcasted_iota(jnp.int32, (B, 2 * B), 0) < lax.broadcasted_iota(jnp.int32, (B, 2 * B), 1)
    sums = jnp.where(before, 1.0, 0.0).astype(bf16)
    valid = jnp.where(z == depth - 1, OUT_ROWS, ALL_ROWS)

    def prepare(c, carry):
        x = jnp.where(row < valid, rows_ref[:, c].astype(f32).reshape(ALL_ROWS, B), 0.0)
        x_ref[...] = x
        square = x * x
        high = square.astype(bf16)
        low = (square - high.astype(f32)).astype(bf16)
        window_sum = windows(dot(x.astype(bf16), sums))
        window_sq = windows(dot(high, sums) + dot(low, sums))
        scales[c] = lax.rsqrt(jnp.maximum(window_sq - window_sum * window_sum / TL, TL / 8.0))
        series[c] = jnp.concatenate([x_ref[b : b + ROWS] for b in range(LAGS)], axis=1).astype(bf16)
        return carry

    lax.fori_loop(0, per, prepare, 0)
    stack[...] = jnp.zeros_like(stack)

    lane = lax.broadcasted_iota(jnp.int32, (OUT_ROWS, B), 1)
    flip_at = lax.broadcasted_iota(jnp.int32, (B, B), 0) + lax.broadcasted_iota(jnp.int32, (B, B), 1)
    flip = jnp.where(flip_at == B - 1, 1.0, 0.0).astype(bf16)
    tpl_all = remote(tpl_ref.at[pl.ds(0, depth - 1)], tpl_ref.at[pl.ds(0, depth - 1)], tpl_sems, self)
    tpl_all.wait_recv()

    def correlate(c, carry):
        half = lax.div(c, 5)
        zero = jnp.zeros((1, B), f32)
        for k in range(K):
            tpl = dot(tpl_ref[2 * k + half, c - 4 * half], flip)
            line = jnp.concatenate([zero] + [tpl[7 - m : 8 - m] for m in range(TPL_ROWS)] + [zero], axis=1)
            for g in range(0, B, 16):
                wide = jnp.broadcast_to(line, (16, line.shape[1]))
                rolled = pltpu.roll(wide, 1 + g, axis=1, stride=1, stride_axis=0).astype(bf16)
                for b in range(LAGS):
                    toeplitz[b * B + g : b * B + g + 16, k * B : (k + 1) * B] = rolled[:, (9 - b) * B : (10 - b) * B]
        correl = dot(series[c], toeplitz[...])
        for k in range(K):
            shift = shifts_ref[k, p * per + c]
            whole = jnp.where(shift >= B, 1, 0)
            rest = shift - whole * B
            moved[k] = pltpu.roll(correl[:, k * B : (k + 1) * B] * scales[c], jnp.where(rest == 0, 0, B - rest), axis=1)
            here, there = moved[k, pl.ds(whole, OUT_ROWS)], moved[k, pl.ds(whole + 1, OUT_ROWS)]
            stack[k] += jnp.where(lane < B - rest, here, there).reshape(GROUP, PIECE, B)
        return carry

    lax.fori_loop(0, per, correlate, 0)

    for i in range(GROUP):
        for j in range(K):
            if i + j > 0:
                q, t = lax.rem(p + i, GROUP), lax.rem(s + j, K)
                remote(stack.at[t, q], from_all.at[p * K + s], stack_sems, {"tm": z * GROUP + q, "sta": t}).start()
    from_all[p * K + s] = stack[s, p]
    senders = GROUP * K - 1
    stack_all = remote(from_all.at[pl.ds(0, senders)], from_all.at[pl.ds(0, senders)], stack_sems, self)
    stack_all.wait_recv()
    total = from_all[0]
    for j in range(1, GROUP * K):
        total += from_all[j]
    peaks[pl.ds(me, 1)] = jnp.max(jnp.abs(total), axis=0, keepdims=True)

    def tell(i, carry):
        mine = peaks.at[pl.ds(me, 1)]
        remote(mine, mine, peak_sems, {"tm": lax.rem(me + i, count), "sta": s}).start()
        return carry

    lax.fori_loop(1, count, tell, 0)
    peak_all = remote(peaks.at[pl.ds(0, count - 1)], peaks.at[pl.ds(0, count - 1)], peak_sems, self)
    peak_all.wait_recv()
    out_ref[...] = total / (jnp.max(peaks[...]) + 1e-06)
    for sent in (bank_all, data_all, part_all, halo, tpl_all, stack_all, peak_all):
        sent.wait_send()


def on_device(data, bank, select, shifts):
    channels = data.shape[0]
    per = channels // GROUP
    tpl_parts = (2 * K, 5, TPL_ROWS, B)
    hbm = pl.BlockSpec(memory_space=pltpu.HBM)
    out = pl.pallas_call(
        kernel,
        out_shape=jax.ShapeDtypeStruct((PIECE, B), f32),
        in_specs=[hbm] * 4,
        out_specs=pl.BlockSpec(memory_space=pltpu.VMEM),
        scratch_shapes=[
            pltpu.SMEM(select.shape, jnp.int32),
            pltpu.SMEM(shifts.shape, jnp.int32),
            pltpu.VMEM(data.shape, bf16),
            pltpu.VMEM(bank.shape[1:], bf16),
            pltpu.VMEM((channels * PIECE, B), f32),
            pltpu.VMEM((channels, PIECE, B), bf16),
            pltpu.VMEM((channels, TPL_ROWS, B), bf16),
            pltpu.VMEM((GROUP + 1, per, PIECE, B), bf16),
            pltpu.VMEM((GROUP, per, TPL_ROWS, B), bf16),
            pltpu.VMEM(tpl_parts, bf16),
            pltpu.VMEM(tpl_parts, bf16),
            pltpu.VMEM(tpl_parts, bf16),
            pltpu.VMEM((ALL_ROWS, B), f32),
            pltpu.VMEM((per, ROWS, B), f32),
            pltpu.VMEM((per, ROWS, LAGS * B), bf16),
            pltpu.VMEM((LAGS * B, K * B), bf16),
            pltpu.VMEM((K, ROWS, B), f32),
            pltpu.VMEM((K, GROUP, PIECE, B), f32),
            pltpu.VMEM((GROUP * K, PIECE, B), f32),
            pltpu.VMEM((lax.axis_size("tm"), B), f32),
            pltpu.SemaphoreType.DMA((4,)),
        ]
        + [pltpu.SemaphoreType.DMA((2,))] * 7,
        compiler_params=pltpu.CompilerParams(
            collective_id=0, has_side_effects=True, vmem_limit_bytes=60 * 2**20
        ),
    )(select, data, bank, shifts)
    return out.reshape(1, PIECE * B)


def solution(mesh):
    in_specs = (P("sta", "tm"), P("tm", "sta", None), P(), P(None, "sta"))
    out_specs = P("sta", "tm")
    return jax.shard_map(on_device, mesh=mesh, in_specs=in_specs, out_specs=out_specs, check_vma=False)
```

time: 1910 us -> 50.7 us (0.03); the launches traced: 1870 us -> 50.6 us
  local copies, waits for them, and re-layouts: 952 us -> 1.3 us
  waiting for transfers between devices: 627 us -> 0 us
  blocking collectives: 193 us -> 0 us
  other arithmetic: 58 us -> 0 us
  Pallas kernels: 0 us -> 49.3 us
    gather x1188 -> x0, local copies, waits for them, and re-layouts: 802 us -> none
    psum x1 -> x0, waiting for transfers between devices: 627 us -> none  [broadcast(): return lax.psum(block, axis)]
    pmax x1 -> x0, blocking collectives: 153 us -> none  [on_device(): peaks = lax.pmax(jnp.max(jnp.abs(summed), axis=1), 'tm')]
    while x684 -> x0, local copies, waits for them, and re-layouts: 67.9 us -> none
    pallas_call x0 -> x1, Pallas kernels: none -> 49.3 us  [on_device(): pl.pallas_call(kernel, out_shape=jax.ShapeDtypeStruct((PIECE, B), f32), i...]
    another operation x72 -> x0, other arithmetic: 42.1 us -> none  [the longest x36 31.9 us: window_sums(): inner_sums = jnp.cumsum(blocks, axis=-1) - blocks]
    psum x1 -> x0, blocking collectives: 39.7 us -> none  [on_device(): summed = lax.psum(partial_stack, 'sta')]
    concatenate x18 -> x0, local copies, waits for them, and re-layouts: 32.9 us -> none  [group_step(): jnp.concatenate([blocked[:, q:q + starts, :] for q in range(lag_padded)],...]
  transfers between devices with their start and end apart: 2 -> 0, of which waited for: 1 -> 0; matrix products, arithmetic and copies ran while one was open for 0% -> 0% of each run, Pallas kernels for 0% -> 0%
where the time goes in v2:
time: 50.7 us; the launch traced here: 50.6 us
  Pallas kernels  49.3 us (97%)
  local copies, waits for them, and re-layouts  1.3 us (3%)
    pallas_call x1, Pallas kernels, on_device(): pl.pallas_call(kernel, out_shape=jax.ShapeDtypeStruct((PIECE, B), f32), i...  49.3 us
    unnamed x1, local copies, waits for them, and re-layouts  1.3 us

profile of v2, /device:TPU:1, one launch (start us, length us, event | category | flops | bytes accessed | tf_op | source)
XLA Modules:
  0.0 50.6 jit_solution(6604686099908576320)
XLA Ops:
  0.0 49.3 %shard_map.46 = f32[16,128]{1,0:T(8,128)} custom-call(s32[4]{0:T(128)} %select_hbm.1, bf16[72,2048]{1,0:T(8,128)(2,1)} %data_hbm.1, bf16[1,72,1024]{2,1,0:T(8,128)(2,1)} %bank_hbm.1, s32[4,72]{1,0:T(4,128)} %shifts_hbm.1), custom_call_target="tpu_custom_call" | custom-call | tf_op jit(solution)/shard_map/pallas_call | solution.py:201
  49.3 1.3 %copy.6 = f32[1,2048]{1,0:T(1,128)} copy(f32[1,2048]{1,0:T(1,128)} %bitcast.1) | data formatting | bytes 16384

commit v3 on v2

--- a/solution.py
+++ b/solution.py
@@ -29,6 +29,16 @@
     )
 
 
+def hops(step, size):
+    return min(step, size - step)
+
+
+def far_first(depth):
+    steps = [(dz, dy, dx) for dz in range(depth) for dy in range(2) for dx in range(4)]
+    length = lambda o: hops(o[0], depth) + 2 * o[1] + hops(o[2], 4)
+    return sorted(steps, key=length, reverse=True)[:-1]
+
+
 def windows(v):
     ahead, total = v[:, :B], v[:, B:]
     two = total[0:143] + total[1:144]
@@ -40,7 +50,7 @@
 def kernel(
     select_hbm, data_hbm, bank_hbm, shifts_hbm, out_ref,
     select_ref, shifts_ref, data_in, bank_in, lay, data_ref, bank_ref, rows_ref, raw, part, got, tpl_ref,
-    x_ref, scales, series, toeplitz, moved, stack, from_all, peaks,
+    x_ref, scales, series, toeplitz, stack, from_all, peaks,
     local_sems, bank_sems, data_sems, part_sems, halo_sems, tpl_sems, stack_sems, peak_sems,
 ):
     me, s = lax.axis_index("tm"), lax.axis_index("sta")
@@ -50,8 +60,14 @@
     p = me - z * GROUP
     per = rows_ref.shape[1]
     self = {"tm": me, "sta": s}
-    group = [lax.rem(p + i, GROUP) for i in range(1, GROUP)]
-    along = [lax.rem(z + i, depth) for i in range(1, depth)]
+    y, x_at = lax.div(p, 4), lax.rem(p, 4)
+
+    def neighbour(dy, dx):
+        return lax.rem(y + dy, 2) * 4 + lax.rem(x_at + dx, 4)
+
+    steps = far_first(depth)
+    group = [neighbour(dy, dx) for dz, dy, dx in steps if dz == 0]
+    along = [lax.rem(z + dz, depth) for dz, dy, dx in steps if dy == dx == 0]
     in_group = lambda q: {"tm": z * GROUP + q, "sta": s}
     in_depth = lambda w: {"tm": w * GROUP + p, "sta": s}
 
@@ -76,6 +92,8 @@
     data_ref[...] = lay[...].astype(bf16).reshape(data_ref.shape)
     loads[2].wait()
     loads[3].wait()
+    flip_at = lax.broadcasted_iota(jnp.int32, (B, B), 0) + lax.broadcasted_iota(jnp.int32, (B, B), 1)
+    flip = jnp.where(flip_at == B - 1, 1.0, 0.0).astype(bf16)
     pl.semaphore_wait(barrier, len(greeted))
 
     for q in group:
@@ -89,10 +107,9 @@
     bank_all.wait_recv()
     for k in range(K):
         wanted = select_ref[k] - z * GROUP
-        picked = jnp.zeros(raw.shape[1:], f32)
-        for j in range(GROUP):
-            picked += jnp.where(wanted == j, raw[j].astype(f32), 0.0)
-        picked = picked.astype(bf16)
+        here = jnp.where((wanted >= 0) & (wanted < GROUP), 1, 0)
+        picked = raw[wanted * here].astype(f32)
+        picked = jnp.where(here == 1, picked, 0.0).astype(bf16)
         for half in range(2):
             part[2 * k + half] = picked[4 * half : 4 * half + 5]
     for w in along:
@@ -112,7 +129,8 @@
     mean = jnp.sum(jnp.sum(tpl, axis=2, keepdims=True), axis=1, keepdims=True) / TL
     centred = tpl - mean
     power = jnp.sum(jnp.sum(centred * centred, axis=2, keepdims=True), axis=1, keepdims=True)
-    tpl_ref[z] = (centred * lax.rsqrt(power + 1e-05)).astype(bf16)
+    normed = (centred * lax.rsqrt(power + 1e-05)).astype(bf16)
+    tpl_ref[z] = dot(normed.reshape(5 * TPL_ROWS, B), flip).astype(bf16).reshape(normed.shape)
     for w in along:
         remote(tpl_ref.at[z], tpl_ref.at[z], tpl_sems, in_depth(w)).start()
 
@@ -138,39 +156,58 @@
     stack[...] = jnp.zeros_like(stack)
 
     lane = lax.broadcasted_iota(jnp.int32, (OUT_ROWS, B), 1)
-    flip_at = lax.broadcasted_iota(jnp.int32, (B, B), 0) + lax.broadcasted_iota(jnp.int32, (B, B), 1)
-    flip = jnp.where(flip_at == B - 1, 1.0, 0.0).astype(bf16)
     tpl_all = remote(tpl_ref.at[pl.ds(0, depth - 1)], tpl_ref.at[pl.ds(0, depth - 1)], tpl_sems, self)
     tpl_all.wait_recv()
 
-    def correlate(c, carry):
-        half = lax.div(c, 5)
-        zero = jnp.zeros((1, B), f32)
+    part_row = lax.broadcasted_iota(jnp.int32, (16, B), 0)
+    part_lane = lax.broadcasted_iota(jnp.int32, (16, B), 1)
+    zero = jnp.zeros((16, B), f32)
+
+    def spread(c, slot):
+        half = jnp.where(c >= 5, 1, 0)
         for k in range(K):
-            tpl = dot(tpl_ref[2 * k + half, c - 4 * half], flip)
-            line = jnp.concatenate([zero] + [tpl[7 - m : 8 - m] for m in range(TPL_ROWS)] + [zero], axis=1)
+            tpl = tpl_ref[2 * k + half, c - 4 * half].astype(f32)
+            lines = [jnp.broadcast_to(tpl[m : m + 1], (16, B)) for m in range(TPL_ROWS)]
             for g in range(0, B, 16):
-                wide = jnp.broadcast_to(line, (16, line.shape[1]))
-                rolled = pltpu.roll(wide, 1 + g, axis=1, stride=1, stride_axis=0).astype(bf16)
+                wraps = part_lane - part_row < 1 + g
+                turned = [pltpu.roll(line, 1 + g, axis=1, stride=1, stride_axis=0) for line in lines]
+                turned = [zero] + turned + [zero]
                 for b in range(LAGS):
-                    toeplitz[b * B + g : b * B + g + 16, k * B : (k + 1) * B] = rolled[:, (9 - b) * B : (10 - b) * B]
-        correl = dot(series[c], toeplitz[...])
+                    block = jnp.where(wraps, turned[b + 1], turned[b])
+                    toeplitz[slot, b * B + g : b * B + g + 16, k * B : (k + 1) * B] = block.astype(bf16)
+
+    def add(c, slot):
+        correl = dot(series[c], toeplitz[slot])
         for k in range(K):
             shift = shifts_ref[k, p * per + c]
-            whole = jnp.where(shift >= B, 1, 0)
-            rest = shift - whole * B
-            moved[k] = pltpu.roll(correl[:, k * B : (k + 1) * B] * scales[c], jnp.where(rest == 0, 0, B - rest), axis=1)
-            here, there = moved[k, pl.ds(whole, OUT_ROWS)], moved[k, pl.ds(whole + 1, OUT_ROWS)]
-            stack[k] += jnp.where(lane < B - rest, here, there).reshape(GROUP, PIECE, B)
+            far = shift >= B
+            rest = jnp.where(far, shift - B, shift)
+            turned = pltpu.roll(correl[:, k * B : (k + 1) * B] * scales[c], jnp.where(rest == 0, 0, B - rest), axis=1)
+            first, second, third = turned[:OUT_ROWS], turned[1 : OUT_ROWS + 1], turned[2 : OUT_ROWS + 2]
+            near_sum = jnp.where(lane < B - rest, first, second)
+            far_sum = jnp.where(lane < B - rest, second, third)
+            stack[k] += jnp.where(far, far_sum, near_sum).reshape(GROUP, PIECE, B)
+
+    spread(0, 0)
+
+    def two_channels(i, carry):
+        c = 2 * i
+        spread(c + 1, 1)
+        add(c, 0)
+        spread(jnp.minimum(c + 2, per - 1), 0)
+        add(c + 1, 1)
         return carry
 
-    lax.fori_loop(0, per, correlate, 0)
-
-    for i in range(GROUP):
-        for j in range(K):
-            if i + j > 0:
-                q, t = lax.rem(p + i, GROUP), lax.rem(s + j, K)
-                remote(stack.at[t, q], from_all.at[p * K + s], stack_sems, {"tm": z * GROUP + q, "sta": t}).start()
+    lax.fori_loop(0, per // 2, two_channels, 0)
+    if per % 2:
+        add(per - 1, 0)
+
+    y_lo, core = lax.div(s, 2), lax.rem(s, 2)
+    ways = [(dy, dx, dl, dc) for dy in range(2) for dx in range(4) for dl in range(2) for dc in range(2)]
+    length = lambda o: (1 if o[2] else 2 * o[0]) + hops(o[1], 4) + 0.1 * o[3]
+    for dy, dx, dl, dc in sorted(ways, key=length, reverse=True)[:-1]:
+        q, t = neighbour(dy, dx), lax.rem(y_lo + dl, 2) * 2 + lax.rem(core + dc, 2)
+        remote(stack.at[t, q], from_all.at[p * K + s], stack_sems, {"tm": z * GROUP + q, "sta": t}).start()
     from_all[p * K + s] = stack[s, p]
     senders = GROUP * K - 1
     stack_all = remote(from_all.at[pl.ds(0, senders)], from_all.at[pl.ds(0, senders)], stack_sems, self)
@@ -180,12 +217,10 @@
         total += from_all[j]
     peaks[pl.ds(me, 1)] = jnp.max(jnp.abs(total), axis=0, keepdims=True)
 
-    def tell(i, carry):
-        mine = peaks.at[pl.ds(me, 1)]
-        remote(mine, mine, peak_sems, {"tm": lax.rem(me + i, count), "sta": s}).start()
-        return carry
-
-    lax.fori_loop(1, count, tell, 0)
+    mine = peaks.at[pl.ds(me, 1)]
+    for dz, dy, dx in steps:
+        device = {"tm": lax.rem(z + dz, depth) * GROUP + neighbour(dy, dx), "sta": s}
+        remote(mine, mine, peak_sems, device).start()
     peak_all = remote(peaks.at[pl.ds(0, count - 1)], peaks.at[pl.ds(0, count - 1)], peak_sems, self)
     peak_all.wait_recv()
     out_ref[...] = total / (jnp.max(peaks[...]) + 1e-06)
@@ -219,8 +254,7 @@
             pltpu.VMEM((ALL_ROWS, B), f32),
             pltpu.VMEM((per, ROWS, B), f32),
             pltpu.VMEM((per, ROWS, LAGS * B), bf16),
-            pltpu.VMEM((LAGS * B, K * B), bf16),
-            pltpu.VMEM((K, ROWS, B), f32),
+            pltpu.VMEM((2, LAGS * B, K * B), bf16),
             pltpu.VMEM((K, GROUP, PIECE, B), f32),
             pltpu.VMEM((GROUP * K, PIECE, B), f32),
             pltpu.VMEM((lax.axis_size("tm"), B), f32),

time: 50.7 us -> 43.2 us (0.85)
  Pallas kernels: 49.3 us -> 41.8 us
    pallas_call x1, Pallas kernels: 49.3 us -> 41.8 us  [on_device(): pl.pallas_call(kernel, out_shape=jax.ShapeDtypeStruct((PIECE, B), f32), i...]
where the time goes in v3:
time: 43.2 us; the launch traced here: 43.1 us
  Pallas kernels  41.8 us (97%)
  local copies, waits for them, and re-layouts  1.3 us (3%)
    pallas_call x1, Pallas kernels, on_device(): pl.pallas_call(kernel, out_shape=jax.ShapeDtypeStruct((PIECE, B), f32), i...  41.8 us
    unnamed x1, local copies, waits for them, and re-layouts  1.3 us

profile of v3, /device:TPU:1, one launch (start us, length us, event | category | flops | bytes accessed | tf_op | source)
XLA Modules:
  0.0 43.1 jit_solution(5871107756394196200)
XLA Ops:
  0.0 41.8 %shard_map.46 = f32[16,128]{1,0:T(8,128)} custom-call(s32[4]{0:T(128)} %select_hbm.1, bf16[72,2048]{1,0:T(8,128)(2,1)} %data_hbm.1, bf16[1,72,1024]{2,1,0:T(8,128)(2,1)} %bank_hbm.1, s32[4,72]{1,0:T(4,128)} %shifts_hbm.1), custom_call_target="tpu_custom_call" | custom-call | tf_op jit(solution)/shard_map/pallas_call | solution.py:236
  41.8 1.3 %copy.6 = f32[1,2048]{1,0:T(1,128)} copy(f32[1,2048]{1,0:T(1,128)} %bitcast.1) | data formatting | bytes 16384

commit v4 on v3

--- a/solution.py
+++ b/solution.py
@@ -51,7 +51,7 @@
     select_hbm, data_hbm, bank_hbm, shifts_hbm, out_ref,
     select_ref, shifts_ref, data_in, bank_in, lay, data_ref, bank_ref, rows_ref, raw, part, got, tpl_ref,
     x_ref, scales, series, toeplitz, stack, from_all, peaks,
-    local_sems, bank_sems, data_sems, part_sems, halo_sems, tpl_sems, stack_sems, peak_sems,
+    local_sems, bank_sems, data_sems, part_sems, halo_sems, stack_sems, peak_sems, tpl_sent, tpl_come,
 ):
     me, s = lax.axis_index("tm"), lax.axis_index("sta")
     count = lax.axis_size("tm")
@@ -71,6 +71,12 @@
     in_group = lambda q: {"tm": z * GROUP + q, "sta": s}
     in_depth = lambda w: {"tm": w * GROUP + p, "sta": s}
 
+    def tpl_copy(w, device):
+        return pltpu.make_async_remote_copy(
+            src_ref=tpl_ref.at[w], dst_ref=tpl_ref.at[w], send_sem=tpl_sent, recv_sem=tpl_come.at[w],
+            device_id=device, device_id_type=MESH,
+        )
+
     barrier = pltpu.get_barrier_semaphore()
     greeted = [in_group(q) for q in group] + [in_depth(w) for w in along]
     greeted += [{"tm": me, "sta": lax.rem(s + i, K)} for i in range(1, K)]
@@ -82,9 +88,15 @@
     for load in loads:
         load.start()
     channels = data_in.shape[0]
+    flip_at = lax.broadcasted_iota(jnp.int32, (B, B), 0) + lax.broadcasted_iota(jnp.int32, (B, B), 1)
+    flip = jnp.where(flip_at == B - 1, 1.0, 0.0).astype(bf16)
     loads[0].wait()
+    rows = bank_in[...].astype(f32)
+    centred = rows - jnp.sum(rows, axis=1, keepdims=True) / TL
+    power = jnp.sum(centred * centred, axis=1, keepdims=True)
+    normed = (centred * lax.rsqrt(power + 1e-05)).astype(bf16)
     for b in range(TPL_ROWS):
-        lay[pl.ds(b, channels, stride=TPL_ROWS), :] = bank_in[:, b * B : (b + 1) * B].astype(f32)
+        lay[pl.ds(b, channels, stride=TPL_ROWS), :] = dot(normed[:, b * B : (b + 1) * B], flip)
     bank_ref[...] = lay[: channels * TPL_ROWS].astype(bf16).reshape(bank_ref.shape)
     loads[1].wait()
     for a in range(PIECE):
@@ -92,8 +104,6 @@
     data_ref[...] = lay[...].astype(bf16).reshape(data_ref.shape)
     loads[2].wait()
     loads[3].wait()
-    flip_at = lax.broadcasted_iota(jnp.int32, (B, B), 0) + lax.broadcasted_iota(jnp.int32, (B, B), 1)
-    flip = jnp.where(flip_at == B - 1, 1.0, 0.0).astype(bf16)
     pl.semaphore_wait(barrier, len(greeted))
 
     for q in group:
@@ -106,12 +116,9 @@
     bank_all = remote(raw.at[pl.ds(0, GROUP - 1)], raw.at[pl.ds(0, GROUP - 1)], bank_sems, self)
     bank_all.wait_recv()
     for k in range(K):
-        wanted = select_ref[k] - z * GROUP
-        here = jnp.where((wanted >= 0) & (wanted < GROUP), 1, 0)
-        picked = raw[wanted * here].astype(f32)
-        picked = jnp.where(here == 1, picked, 0.0).astype(bf16)
-        for half in range(2):
-            part[2 * k + half] = picked[4 * half : 4 * half + 5]
+        offered = raw[lax.rem(select_ref[k], GROUP)]
+        part[2 * k] = offered[:5]
+        part[2 * k + 1] = offered[4:]
     for w in along:
         remote(part.at[w], got.at[z], part_sems, in_depth(w)).start()
     got[z] = part[z]
@@ -123,16 +130,36 @@
 
     part_all = remote(got.at[pl.ds(0, depth - 1)], got.at[pl.ds(0, depth - 1)], part_sems, self)
     part_all.wait_recv()
-    tpl = got[0].astype(f32)
-    for j in range(1, GROUP):
-        tpl += got[j].astype(f32)
-    mean = jnp.sum(jnp.sum(tpl, axis=2, keepdims=True), axis=1, keepdims=True) / TL
-    centred = tpl - mean
-    power = jnp.sum(jnp.sum(centred * centred, axis=2, keepdims=True), axis=1, keepdims=True)
-    normed = (centred * lax.rsqrt(power + 1e-05)).astype(bf16)
-    tpl_ref[z] = dot(normed.reshape(5 * TPL_ROWS, B), flip).astype(bf16).reshape(normed.shape)
+    tpl_ref[z] = got[lax.div(select_ref[lax.div(z, 2)], GROUP)]
     for w in along:
-        remote(tpl_ref.at[z], tpl_ref.at[z], tpl_sems, in_depth(w)).start()
+        tpl_copy(z, in_depth(w)).start()
+
+    part_row = lax.broadcasted_iota(jnp.int32, (16, B), 0)
+    part_lane = lax.broadcasted_iota(jnp.int32, (16, B), 1)
+    zero = jnp.zeros((16, B), f32)
+
+    def spread_one(tpl, c, k):
+        tpl = tpl.astype(f32)
+        lines = [jnp.broadcast_to(tpl[m : m + 1], (16, B)) for m in range(TPL_ROWS)]
+        for g in range(0, B, 16):
+            wraps = part_lane - part_row < 1 + g
+            turned = [pltpu.roll(line, 1 + g, axis=1, stride=1, stride_axis=0) for line in lines]
+            turned = [zero] + turned + [zero]
+            for b in range(LAGS):
+                block = jnp.where(wraps, turned[b + 1], turned[b])
+                toeplitz[c, k, b * B + g : b * B + g + 16] = block.astype(bf16)
+
+    def spread(w):
+        k = lax.div(w, 2)
+        half = w - 2 * k
+        for i in range(4):
+            spread_one(tpl_ref[w, i + half], 5 * half + i, k)
+
+        @pl.when(half == 0)
+        def _():
+            spread_one(tpl_ref[w, 4], 4, k)
+
+    spread(z)
 
     halo.wait_recv()
     row = lax.broadcasted_iota(jnp.int32, (ALL_ROWS, B), 0)
@@ -156,58 +183,49 @@
     stack[...] = jnp.zeros_like(stack)
 
     lane = lax.broadcasted_iota(jnp.int32, (OUT_ROWS, B), 1)
-    tpl_all = remote(tpl_ref.at[pl.ds(0, depth - 1)], tpl_ref.at[pl.ds(0, depth - 1)], tpl_sems, self)
-    tpl_all.wait_recv()
-
-    part_row = lax.broadcasted_iota(jnp.int32, (16, B), 0)
-    part_lane = lax.broadcasted_iota(jnp.int32, (16, B), 1)
-    zero = jnp.zeros((16, B), f32)
-
-    def spread(c, slot):
-        half = jnp.where(c >= 5, 1, 0)
+
+    def arrive(i, carry):
+        away = jnp.where(lax.rem(i, 2) == 1, lax.div(i + 1, 2), depth - lax.div(i, 2))
+        w = lax.rem(z + away, depth)
+        tpl_copy(w, self).wait_recv()
+        spread(w)
+        return carry
+
+    lax.fori_loop(1, depth, arrive, 0)
+
+    def correlate(c):
+        return dot(series[c], jnp.concatenate([toeplitz[c, k] for k in range(K)], axis=1))
+
+    def add(c, k, correl):
+        shift = shifts_ref[k, p * per + c]
+        far = shift >= B
+        rest = jnp.where(far, shift - B, shift)
+        turned = pltpu.roll(correl[:, k * B : (k + 1) * B] * scales[c], jnp.where(rest == 0, 0, B - rest), axis=1)
+        first, second, third = turned[:OUT_ROWS], turned[1 : OUT_ROWS + 1], turned[2 : OUT_ROWS + 2]
+        near_sum = jnp.where(lane < B - rest, first, second)
+        far_sum = jnp.where(lane < B - rest, second, third)
+        stack[k] += jnp.where(far, far_sum, near_sum).reshape(GROUP, PIECE, B)
+
+    def channel(c, carry):
+        correl = correlate(c)
         for k in range(K):
-            tpl = tpl_ref[2 * k + half, c - 4 * half].astype(f32)
-            lines = [jnp.broadcast_to(tpl[m : m + 1], (16, B)) for m in range(TPL_ROWS)]
-            for g in range(0, B, 16):
-                wraps = part_lane - part_row < 1 + g
-                turned = [pltpu.roll(line, 1 + g, axis=1, stride=1, stride_axis=0) for line in lines]
-                turned = [zero] + turned + [zero]
-                for b in range(LAGS):
-                    block = jnp.where(wraps, turned[b + 1], turned[b])
-                    toeplitz[slot, b * B + g : b * B + g + 16, k * B : (k + 1) * B] = block.astype(bf16)
-
-    def add(c, slot):
-        correl = dot(series[c], toeplitz[slot])
-        for k in range(K):
-            shift = shifts_ref[k, p * per + c]
-            far = shift >= B
-            rest = jnp.where(far, shift - B, shift)
-            turned = pltpu.roll(correl[:, k * B : (k + 1) * B] * scales[c], jnp.where(rest == 0, 0, B - rest), axis=1)
-            first, second, third = turned[:OUT_ROWS], turned[1 : OUT_ROWS + 1], turned[2 : OUT_ROWS + 2]
-            near_sum = jnp.where(lane < B - rest, first, second)
-            far_sum = jnp.where(lane < B - rest, second, third)
-            stack[k] += jnp.where(far, far_sum, near_sum).reshape(GROUP, PIECE, B)
-
-    spread(0, 0)
-
-    def two_channels(i, carry):
-        c = 2 * i
-        spread(c + 1, 1)
-        add(c, 0)
-        spread(jnp.minimum(c + 2, per - 1), 0)
-        add(c + 1, 1)
+            add(c, k, correl)
         return carry
 
-    lax.fori_loop(0, per // 2, two_channels, 0)
-    if per % 2:
-        add(per - 1, 0)
-
-    y_lo, core = lax.div(s, 2), lax.rem(s, 2)
-    ways = [(dy, dx, dl, dc) for dy in range(2) for dx in range(4) for dl in range(2) for dc in range(2)]
-    length = lambda o: (1 if o[2] else 2 * o[0]) + hops(o[1], 4) + 0.1 * o[3]
-    for dy, dx, dl, dc in sorted(ways, key=length, reverse=True)[:-1]:
-        q, t = neighbour(dy, dx), lax.rem(y_lo + dl, 2) * 2 + lax.rem(core + dc, 2)
-        remote(stack.at[t, q], from_all.at[p * K + s], stack_sems, {"tm": z * GROUP + q, "sta": t}).start()
+    lax.fori_loop(0, per - 1, channel, 0, unroll=4)
+
+    correl = correlate(per - 1)
+    for k in range(K):
+        add(per - 1, k, correl)
+        for dz, dy, dx in steps:
+            if dz == 0:
+                q = neighbour(dy, dx)
+                remote(stack.at[k, q], from_all.at[p * K + s], stack_sems, {"tm": z * GROUP + q, "sta": k}).start()
+
+        @pl.when(s != k)
+        def _():
+            remote(stack.at[k, p], from_all.at[p * K + s], stack_sems, {"tm": me, "sta": k}).start()
+
     from_all[p * K + s] = stack[s, p]
     senders = GROUP * K - 1
     stack_all = remote(from_all.at[pl.ds(0, senders)], from_all.at[pl.ds(0, senders)], stack_sems, self)
@@ -224,7 +242,9 @@
     peak_all = remote(peaks.at[pl.ds(0, count - 1)], peaks.at[pl.ds(0, count - 1)], peak_sems, self)
     peak_all.wait_recv()
     out_ref[...] = total / (jnp.max(peaks[...]) + 1e-06)
-    for sent in (bank_all, data_all, part_all, halo, tpl_all, stack_all, peak_all):
+    tpl_all = pltpu.make_async_copy(tpl_ref.at[pl.ds(0, depth - 1)], tpl_ref.at[pl.ds(0, depth - 1)], tpl_sent)
+    tpl_all.wait()
+    for sent in (bank_all, data_all, part_all, halo, stack_all, peak_all):
         sent.wait_send()
 
 
@@ -254,13 +274,14 @@
             pltpu.VMEM((ALL_ROWS, B), f32),
             pltpu.VMEM((per, ROWS, B), f32),
             pltpu.VMEM((per, ROWS, LAGS * B), bf16),
-            pltpu.VMEM((2, LAGS * B, K * B), bf16),
+            pltpu.VMEM((per, K, LAGS * B, B), bf16),
             pltpu.VMEM((K, GROUP, PIECE, B), f32),
             pltpu.VMEM((GROUP * K, PIECE, B), f32),
             pltpu.VMEM((lax.axis_size("tm"), B), f32),
             pltpu.SemaphoreType.DMA((4,)),
         ]
-        + [pltpu.SemaphoreType.DMA((2,))] * 7,
+        + [pltpu.SemaphoreType.DMA((2,))] * 6
+        + [pltpu.SemaphoreType.DMA, pltpu.SemaphoreType.DMA((2 * K,))],
         compiler_params=pltpu.CompilerParams(
             collective_id=0, has_side_effects=True, vmem_limit_bytes=60 * 2**20
         ),

time: 43.2 us -> 42.7 us (0.988)
  Pallas kernels: 41.8 us -> 41.2 us
    pallas_call x1, Pallas kernels: 41.8 us -> 41.2 us  [on_device(): pl.pallas_call(kernel, out_shape=jax.ShapeDtypeStruct((PIECE, B), f32), i...]
where the time goes in v4:
time: 42.7 us; the launch traced here: 42.5 us
  Pallas kernels  41.2 us (96%)
  local copies, waits for them, and re-layouts  1.3 us (3%)
    pallas_call x1, Pallas kernels, on_device(): pl.pallas_call(kernel, out_shape=jax.ShapeDtypeStruct((PIECE, B), f32), i...  41.2 us
    unnamed x1, local copies, waits for them, and re-layouts  1.3 us

profile of v4, /device:TPU:1, one launch (start us, length us, event | category | flops | bytes accessed | tf_op | source)
XLA Modules:
  0.0 42.5 jit_solution(4563533591442339822)
XLA Ops:
  0.0 41.2 %shard_map.46 = f32[16,128]{1,0:T(8,128)} custom-call(s32[4]{0:T(128)} %select_hbm.1, bf16[72,2048]{1,0:T(8,128)(2,1)} %data_hbm.1, bf16[1,72,1024]{2,1,0:T(8,128)(2,1)} %bank_hbm.1, s32[4,72]{1,0:T(4,128)} %shifts_hbm.1), custom_call_target="tpu_custom_call" | custom-call | tf_op jit(solution)/shard_map/pallas_call | solution.py:256
  41.3 1.3 %copy.6 = f32[1,2048]{1,0:T(1,128)} copy(f32[1,2048]{1,0:T(1,128)} %bitcast.1) | data formatting | bytes 16384

commit v5 on v4

--- a/solution.py
+++ b/solution.py
@@ -77,16 +77,16 @@
             device_id=device, device_id_type=MESH,
         )
 
-    barrier = pltpu.get_barrier_semaphore()
-    greeted = [in_group(q) for q in group] + [in_depth(w) for w in along]
-    greeted += [{"tm": me, "sta": lax.rem(s + i, K)} for i in range(1, K)]
-    for device in greeted:
-        pl.semaphore_signal(barrier, inc=1, device_id=device, device_id_type=MESH)
-
     inputs = [(bank_hbm.at[0], bank_in), (data_hbm, data_in), (select_hbm, select_ref), (shifts_hbm, shifts_ref)]
     loads = [pltpu.make_async_copy(src, dst, local_sems.at[i]) for i, (src, dst) in enumerate(inputs)]
     for load in loads:
         load.start()
+    barrier = pltpu.get_barrier_semaphore()
+    greeted = [in_depth(w) for w in along] + [in_group(q) for q in group]
+    greeted += [{"tm": me, "sta": lax.rem(s + i, K)} for i in range(1, K)]
+    for device in greeted:
+        pl.semaphore_signal(barrier, inc=1, device_id=device, device_id_type=MESH)
+
     channels = data_in.shape[0]
     flip_at = lax.broadcasted_iota(jnp.int32, (B, B), 0) + lax.broadcasted_iota(jnp.int32, (B, B), 1)
     flip = jnp.where(flip_at == B - 1, 1.0, 0.0).astype(bf16)
@@ -98,21 +98,21 @@
     for b in range(TPL_ROWS):
         lay[pl.ds(b, channels, stride=TPL_ROWS), :] = dot(normed[:, b * B : (b + 1) * B], flip)
     bank_ref[...] = lay[: channels * TPL_ROWS].astype(bf16).reshape(bank_ref.shape)
+    pl.semaphore_wait(barrier, len(greeted))
+
+    for q in group:
+        remote(bank_ref.at[pl.ds(q * per, per)], raw.at[p], bank_sems, in_group(q)).start()
     loads[1].wait()
     for a in range(PIECE):
         lay[pl.ds(a, channels, stride=PIECE), :] = data_in[:, a * B : (a + 1) * B].astype(f32)
     data_ref[...] = lay[...].astype(bf16).reshape(data_ref.shape)
-    loads[2].wait()
-    loads[3].wait()
-    pl.semaphore_wait(barrier, len(greeted))
-
-    for q in group:
-        remote(bank_ref.at[pl.ds(q * per, per)], raw.at[p], bank_sems, in_group(q)).start()
-    for q in group:
+    for q in group[::-1]:
         remote(data_ref.at[pl.ds(q * per, per)], rows_ref.at[p], data_sems, in_group(q)).start()
     raw[p] = bank_ref[pl.ds(p * per, per)]
     rows_ref[p] = data_ref[pl.ds(p * per, per)]
 
+    loads[2].wait()
+    loads[3].wait()
     bank_all = remote(raw.at[pl.ds(0, GROUP - 1)], raw.at[pl.ds(0, GROUP - 1)], bank_sems, self)
     bank_all.wait_recv()
     for k in range(K):
@@ -212,7 +212,7 @@
             add(c, k, correl)
         return carry
 
-    lax.fori_loop(0, per - 1, channel, 0, unroll=4)
+    lax.fori_loop(0, per - 1, channel, 0, unroll=True)
 
     correl = correlate(per - 1)
     for k in range(K):

time: 42.7 us -> 41.9 us (0.981)
  Pallas kernels: 41.2 us -> 40.4 us
    pallas_call x1, Pallas kernels: 41.2 us -> 40.4 us  [on_device(): pl.pallas_call(kernel, out_shape=jax.ShapeDtypeStruct((PIECE, B), f32), i...]
where the time goes in v5:
time: 41.9 us; the launch traced here: 41.7 us
  Pallas kernels  40.4 us (96%)
  local copies, waits for them, and re-layouts  1.3 us (3%)
    pallas_call x1, Pallas kernels, on_device(): pl.pallas_call(kernel, out_shape=jax.ShapeDtypeStruct((PIECE, B), f32), i...  40.4 us
    unnamed x1, local copies, waits for them, and re-layouts  1.3 us

profile of v5, /device:TPU:1, one launch (start us, length us, event | category | flops | bytes accessed | tf_op | source)
XLA Modules:
  0.0 41.7 jit_solution(7253045982963136033)
XLA Ops:
  0.0 40.4 %shard_map.46 = f32[16,128]{1,0:T(8,128)} custom-call(s32[4]{0:T(128)} %select_hbm.1, bf16[72,2048]{1,0:T(8,128)(2,1)} %data_hbm.1, bf16[1,72,1024]{2,1,0:T(8,128)(2,1)} %bank_hbm.1, s32[4,72]{1,0:T(4,128)} %shifts_hbm.1), custom_call_target="tpu_custom_call" | custom-call | tf_op jit(solution)/shard_map/pallas_call | solution.py:256
  40.4 1.3 %copy.6 = f32[1,2048]{1,0:T(1,128)} copy(f32[1,2048]{1,0:T(1,128)} %bitcast.1) | data formatting | bytes 16384

commit v6 on v5

--- a/solution.py
+++ b/solution.py
@@ -283,7 +283,7 @@
         + [pltpu.SemaphoreType.DMA((2,))] * 6
         + [pltpu.SemaphoreType.DMA, pltpu.SemaphoreType.DMA((2 * K,))],
         compiler_params=pltpu.CompilerParams(
-            collective_id=0, has_side_effects=True, vmem_limit_bytes=60 * 2**20
+            collective_id=0, has_side_effects=True, vmem_limit_bytes=int(53.8 * 2**20)
         ),
     )(select, data, bank, shifts)
     return out.reshape(1, PIECE * B)

time: 41.9 us -> 41.9 us (level)
  local copies, waits for them, and re-layouts: 1.3 us -> 1.94 us
  Pallas kernels: 40.4 us -> 39.8 us
    unnamed x1 -> x5, local copies, waits for them, and re-layouts: 1.3 us -> 1.94 us
    pallas_call x1, Pallas kernels: 40.4 us -> 39.8 us  [on_device(): pl.pallas_call(kernel, out_shape=jax.ShapeDtypeStruct((PIECE, B), f32), i...]
where the time goes in v6:
time: 41.9 us; the launch traced here: 41.8 us
  Pallas kernels  39.8 us (95%)
  local copies, waits for them, and re-layouts  1.94 us (5%)
    pallas_call x1, Pallas kernels, on_device(): pl.pallas_call(kernel, out_shape=jax.ShapeDtypeStruct((PIECE, B), f32), i...  39.8 us
    unnamed x5, local copies, waits for them, and re-layouts  1.94 us

profile of v6, /device:TPU:1, one launch (start us, length us, event | category | flops | bytes accessed | tf_op | source)
XLA Modules:
  0.0 41.8 jit_solution(8315559349974578994)
XLA Ops:
  0.0 0.0 copy-start
  0.0 0.7 %copy-done = s32[4,72]{1,0:T(4,128)S(1)} copy-done((s32[4,72]{1,0:T(4,128)S(1)}, s32[4,72]{1,0:T(4,128)}, u32[]{:S(2)}) %copy-start) | copy-done | bytes 1176
  0.7 0.0 copy-start.1
  0.7 0.7 %copy-done.1 = s32[4]{0:T(128)S(1)} copy-done((s32[4]{0:T(128)S(1)}, s32[4]{0:T(128)}, u32[]{:S(2)}) %copy-start.1) | copy-done | bytes 40
  1.3 39.8 %shard_map.46 = f32[16,128]{1,0:T(8,128)S(1)} custom-call(s32[4]{0:T(128)S(1)} %copy-done.1, bf16[72,2048]{1,0:T(8,128)(2,1)} %data_hbm.1, bf16[1,72,1024]{2,1,0:T(8,128)(2,1)} %bank_hbm.1, s32[4,72]{1,0:T(4,128)S(1)} %copy-done), custom_call_target="tpu_custom_call" | custom-call | tf_op jit(solution)/shard_map/pallas_call | solution.py:256
  41.2 0.6 %copy.6 = f32[1,2048]{1,0:T(1,128)} copy(f32[1,2048]{1,0:T(1,128)S(1)} %bitcast.1) | data formatting | bytes 16384
Async XLA Ops:
  0.0 0.7 %copy-start = (s32[4,72]{1,0:T(4,128)S(1)}, s32[4,72]{1,0:T(4,128)}, u32[]{:S(2)}) copy-start(s32[4,72]{1,0:T(4,128)} %shifts_hbm.1) | copy-start | bytes 3460
  0.7 0.7 %copy-start.1 = (s32[4]{0:T(128)S(1)}, s32[4]{0:T(128)}, u32[]{:S(2)}) copy-start(s32[4]{0:T(128)} %select_hbm.1) | copy-start | bytes 52
